TPU v7x, 32 devices: a whole 2x2x4 slice. The times are simulated.
32 devices in a mesh: dp: 4 (over z), ctx: 2 (over y), tensor: 4 (over x, core).
Axes of the slice: x: 2, y: 2, z: 4, core: 2. Of those that a mesh axis runs over, the one named last changes fastest.
Arguments:
- tokens: bfloat16 [16384, 1024], P(('dp', 'ctx', 'tensor')), may hold values from -6 to 6
- segment_ids: int32 [16384], P('dp'), may hold values from 0 to 3, as said below
- w_query: bfloat16 [1024, 2048], P(('dp', 'ctx'), 'tensor'), may hold values from -0.1875 to 0.1875
- key_matrix: bfloat16 [1024, 1024], P(('dp', 'ctx'), 'tensor'), may hold values from -0.1875 to 0.1875
- value_matrix: bfloat16 [1024, 1024], P(('dp', 'ctx'), 'tensor'), may hold values from -0.1875 to 0.1875
- w_out: bfloat16 [2048, 1024], P('tensor', ('dp', 'ctx')), may hold values from -2 to 2
- w_gate: bfloat16 [1024, 3072], P(('dp', 'ctx'), 'tensor'), may hold values from -0.1875 to 0.1875
- w_up: bfloat16 [1024, 3072], P(('dp', 'ctx'), 'tensor'), may hold values from -0.1875 to 0.1875
- w_down: bfloat16 [3072, 1024], P('tensor', ('dp', 'ctx')), may hold values from -0.109375 to 0.109375
- gain_attn: bfloat16 [1024], P(('dp', 'ctx')), may hold values from 0.5 to 1.5
- gain_mlp: bfloat16 [1024], P(('dp', 'ctx')), may hold values from 0.5 to 1.5
- gain_query: bfloat16 [128], P(('dp', 'ctx')), may hold values from 0.5 to 1.5
- gain_key: bfloat16 [128], P(('dp', 'ctx')), may hold values from 0.5 to 1.5
- out_cot: bfloat16 [16384, 1024], P(('dp', 'ctx', 'tensor')), may hold values from -6 to 6
Outputs:
- layer_out: bfloat16 [16384, 1024], P(('dp', 'ctx', 'tensor'))
- d_tokens: bfloat16 [16384, 1024], P(('dp', 'ctx', 'tensor'))
- grad_w_query: float32 [1024, 2048], P(('dp', 'ctx'), 'tensor')
- grad_w_key: float32 [1024, 1024], P(('dp', 'ctx'), 'tensor')
- grad_w_value: float32 [1024, 1024], P(('dp', 'ctx'), 'tensor')
- grad_w_out: float32 [2048, 1024], P('tensor', ('dp', 'ctx'))
- grad_w_gate: float32 [1024, 3072], P(('dp', 'ctx'), 'tensor')
- grad_w_up: float32 [1024, 3072], P(('dp', 'ctx'), 'tensor')
- grad_w_down: float32 [3072, 1024], P('tensor', ('dp', 'ctx'))
- grad_gain_attn: float32 [1024], P(('dp', 'ctx'))
- grad_gain_mlp: float32 [1024], P(('dp', 'ctx'))
- grad_gain_query: float32 [128], P(('dp', 'ctx'))
- grad_gain_key: float32 [128], P(('dp', 'ctx'))
Inputs may be any that keep to these rules, and one draw needn't show every extreme that they name: `segment_ids`: within each data group of 4096 tokens the ids never fall, the first token has id 0 and the last id 3; one segment holds token 2047 and token 2048 of its group.
All inputs are finite; a program needn't handle non-finite values.
Results may differ from a plain program's by a relative error of at most 0.024.
Values may be sent and summed in bfloat16 or wider, within the bound.
A program may use at most 256 MiB of HBM per device.

v0:
```python
from functools import partial

import jax
import jax.numpy as jnp
from jax import lax
from jax.sharding import PartitionSpec as P

HEAD_SIZE = 128


EPS = 1e-06
THETA = 1000000.0


def from_behind(shard, axis, by):
    length = lax.axis_size(axis)
    pairs = [(i, i + by) for i in range(length) if 0 <= i + by < length]
    return lax.ppermute(shard, axis, pairs)


def norm_rows(field, gain):
    return field * lax.rsqrt(jnp.mean(field * field, axis=-1, keepdims=True) + EPS) * gain


def norm_back(field, gain, incoming):
    inverse = lax.rsqrt(jnp.mean(field * field, axis=-1, keepdims=True) + EPS)
    scaled = incoming * gain
    d_field = inverse * scaled - field * (inverse * inverse * inverse) * jnp.mean(
        scaled * field, axis=-1, keepdims=True
    )
    return (d_field, incoming * field * inverse)


def rotary_tables(segment):
    length_total = segment.shape[0]
    positions = jnp.arange(length_total, dtype=jnp.int32)
    begins = jnp.concatenate([jnp.ones((1,), dtype=jnp.bool_), segment[1:] != segment[:-1]])
    starts = lax.cummax(jnp.where(begins, positions, jnp.zeros_like(positions)), axis=0)
    offset = (positions - starts).astype(jnp.float32)
    frequency = THETA ** (-2.0 * jnp.arange(HEAD_SIZE // 2, dtype=jnp.float32) / HEAD_SIZE)
    angles = offset[:, None] * frequency[None, :]
    cosine_table = jnp.cos(angles)
    sine_table = jnp.sin(angles)
    return (
        jnp.concatenate([cosine_table, cosine_table], axis=-1),
        jnp.concatenate([sine_table, sine_table], axis=-1),
    )


def rotate(field, cosine_table, sine_table):
    midpoint = field.shape[-1] // 2
    turned = jnp.concatenate([-field[..., midpoint:], field[..., :midpoint]], axis=-1)
    return field * cosine_table + turned * sine_table


def rotate_back(field, cosine_table, sine_table):
    midpoint = field.shape[-1] // 2
    turned = field * sine_table
    return field * cosine_table + jnp.concatenate(
        [turned[..., midpoint:], -turned[..., :midpoint]], axis=-1
    )


def block_scores(
    query_part, segment_part, position_part, key_rows, key_segment, key_position, scaling
):
    scores = (
        jnp.einsum("qhgd,khd->hgqk", query_part, key_rows, preferred_element_type=jnp.float32)
        * scaling
    )
    allowed = (segment_part[:, None] == key_segment[None, :]) & (
        key_position[None, :] <= position_part[:, None]
    )
    return jnp.where(allowed, scores, -1e30)


def rows_first(left, right):
    return lax.dot_general(
        left, right, (((0,), (0,)), ((), ())), preferred_element_type=jnp.float32
    )


def rows_last(left, right):
    return lax.dot_general(
        left, right, (((1,), (1,)), ((), ())), preferred_element_type=jnp.float32
    )


def per_device(
    tokens,
    segment_ids,
    w_query,
    key_matrix,
    value_matrix,
    w_out,
    w_gate,
    w_up,
    w_down,
    gain_attn,
    gain_mlp,
    gain_query,
    gain_key,
    out_cot,
):
    gathered = (
        lax.all_gather(w_query, ("dp", "ctx"), axis=0, tiled=True),
        lax.all_gather(key_matrix, ("dp", "ctx"), axis=0, tiled=True),
        lax.all_gather(value_matrix, ("dp", "ctx"), axis=0, tiled=True),
        lax.all_gather(w_out, ("dp", "ctx"), axis=1, tiled=True),
        lax.all_gather(w_gate, ("dp", "ctx"), axis=0, tiled=True),
        lax.all_gather(w_up, ("dp", "ctx"), axis=0, tiled=True),
        lax.all_gather(w_down, ("dp", "ctx"), axis=1, tiled=True),
        lax.all_gather(gain_attn, ("dp", "ctx"), axis=0, tiled=True),
        lax.all_gather(gain_mlp, ("dp", "ctx"), axis=0, tiled=True),
        lax.all_gather(gain_query, ("dp", "ctx"), axis=0, tiled=True),
        lax.all_gather(gain_key, ("dp", "ctx"), axis=0, tiled=True),
    )
    full_query, full_key, full_value, full_out = (
        gathered[0],
        gathered[1],
        gathered[2],
        gathered[3],
    )
    full_gate, full_up, full_down = (gathered[4], gathered[5], gathered[6])
    attn_gain = gathered[7].astype(jnp.float32)
    mlp_gain = gathered[8].astype(jnp.float32)
    query_gain = gathered[9].astype(jnp.float32)
    key_gain = gathered[10].astype(jnp.float32)
    q_heads = full_query.shape[1] // HEAD_SIZE
    kv_heads = full_key.shape[1] // HEAD_SIZE
    sharing_count = q_heads // kv_heads
    scaling = HEAD_SIZE ** (-0.5)
    ctx_index = lax.axis_index("ctx")
    rows_in = tokens.astype(jnp.float32)
    first_norm = norm_rows(rows_in, attn_gain).astype(jnp.bfloat16)
    norm_one_all = lax.all_gather(first_norm, "tensor", axis=0, tiled=True)
    span = norm_one_all.shape[0]
    cosine_all, sine_all = rotary_tables(segment_ids)
    cosine_table = lax.dynamic_slice_in_dim(cosine_all, ctx_index * span, span, 0)[:, None, :]
    sine_table = lax.dynamic_slice_in_dim(sine_all, ctx_index * span, span, 0)[:, None, :]
    q_linear = jnp.dot(norm_one_all, full_query, preferred_element_type=jnp.float32).reshape(
        span, q_heads, HEAD_SIZE
    )
    key_linear = jnp.dot(norm_one_all, full_key, preferred_element_type=jnp.float32).reshape(
        span, kv_heads, HEAD_SIZE
    )
    value_rows = (
        jnp.dot(norm_one_all, full_value, preferred_element_type=jnp.float32)
        .astype(jnp.bfloat16)
        .reshape(span, kv_heads, HEAD_SIZE)
    )
    query_rows = rotate(norm_rows(q_linear, query_gain), cosine_table, sine_table).astype(
        jnp.bfloat16
    )
    key_rows = rotate(norm_rows(key_linear, key_gain), cosine_table, sine_table).astype(
        jnp.bfloat16
    )
    prev_key_rows, prev_values = from_behind((key_rows, value_rows), "ctx", 1)
    all_keys = jnp.concatenate([prev_key_rows, key_rows], axis=0)
    all_values = jnp.concatenate([prev_values, value_rows], axis=0)
    key_position = (ctx_index - 1) * span + jnp.arange(2 * span, dtype=jnp.int32)
    padded_segment = jnp.concatenate([jnp.full((span,), -1, jnp.int32), segment_ids])
    key_segment = lax.dynamic_slice_in_dim(padded_segment, ctx_index * span, 2 * span, 0)
    query_segment = lax.dynamic_slice_in_dim(segment_ids, ctx_index * span, span, 0)
    query_position = ctx_index * span + jnp.arange(span, dtype=jnp.int32)
    block_length = min(512, span)
    block_count = span // block_length
    query_tiles = query_rows.reshape(block_count, block_length, kv_heads, sharing_count, HEAD_SIZE)
    segment_blocks = query_segment.reshape(block_count, block_length)
    position_blocks = query_position.reshape(block_count, block_length)

    def attend_forward(use_prev):
        begin = 0 if use_prev else span
        outcomes = []
        logs = []
        for index in range(block_count):
            finish = span + (index + 1) * block_length
            scores = block_scores(
                query_tiles[index],
                segment_blocks[index],
                position_blocks[index],
                all_keys[begin:finish],
                key_segment[begin:finish],
                key_position[begin:finish],
                scaling,
            )
            highest = jnp.max(scores, axis=-1, keepdims=True)
            expanded = jnp.exp(scores - highest)
            totals = jnp.sum(expanded, axis=-1, keepdims=True)
            weights = (expanded / totals).astype(jnp.bfloat16)
            outcomes.append(
                jnp.einsum(
                    "hgqk,khd->qhgd",
                    weights,
                    all_values[begin:finish],
                    preferred_element_type=jnp.float32,
                )
            )
            logs.append((highest + jnp.log(totals))[..., 0])
        return (jnp.concatenate(outcomes, axis=0), jnp.stack(logs, axis=0))

    attn_blocks, log_totals = lax.cond(
        ctx_index > 0, partial(attend_forward, True), partial(attend_forward, False)
    )
    attn_float = attn_blocks.reshape(span, q_heads * HEAD_SIZE)
    attn_low = attn_float.astype(jnp.bfloat16)
    attn_part = jnp.dot(attn_low, full_out, preferred_element_type=jnp.float32)
    attn_total = lax.psum_scatter(
        attn_part.astype(jnp.bfloat16), "tensor", scatter_dimension=0, tiled=True
    ).astype(jnp.float32)
    middle = rows_in + attn_total
    norm_two = norm_rows(middle, mlp_gain).astype(jnp.bfloat16)
    norm_two_all = lax.all_gather(norm_two, "tensor", axis=0, tiled=True)
    gate_act = jnp.dot(norm_two_all, full_gate, preferred_element_type=jnp.float32)
    up_proj = jnp.dot(norm_two_all, full_up, preferred_element_type=jnp.float32)
    hidden = (jax.nn.silu(gate_act) * up_proj).astype(jnp.bfloat16)
    mlp_total = lax.psum_scatter(
        jnp.dot(hidden, full_down, preferred_element_type=jnp.float32).astype(jnp.bfloat16),
        "tensor",
        scatter_dimension=0,
        tiled=True,
    ).astype(jnp.float32)
    layer_out = (middle + mlp_total).astype(jnp.bfloat16)
    again = (
        lax.all_gather(w_query, ("dp", "ctx"), axis=0, tiled=True),
        lax.all_gather(key_matrix, ("dp", "ctx"), axis=0, tiled=True),
        lax.all_gather(value_matrix, ("dp", "ctx"), axis=0, tiled=True),
        lax.all_gather(w_out, ("dp", "ctx"), axis=1, tiled=True),
        lax.all_gather(w_gate, ("dp", "ctx"), axis=0, tiled=True),
        lax.all_gather(w_up, ("dp", "ctx"), axis=0, tiled=True),
        lax.all_gather(w_down, ("dp", "ctx"), axis=1, tiled=True),
    )
    back_query, back_key, back_value, back_out = (again[0], again[1], again[2], again[3])
    back_gate, back_up, back_down = (again[4], again[5], again[6])
    cot_all = lax.all_gather(out_cot, "tensor", axis=0, tiled=True)
    grad_down = rows_first(hidden, cot_all)
    d_hidden = rows_last(cot_all, back_down)
    sigma_gate = jax.nn.sigmoid(gate_act)
    d_gate = (d_hidden * up_proj * sigma_gate * (1.0 + gate_act * (1.0 - sigma_gate))).astype(
        jnp.bfloat16
    )
    d_up = (d_hidden * gate_act * sigma_gate).astype(jnp.bfloat16)
    grad_gate = rows_first(norm_two_all, d_gate)
    grad_up = rows_first(norm_two_all, d_up)
    d_two_part = rows_last(d_gate, back_gate) + rows_last(d_up, back_up)
    d_norm_two = lax.psum_scatter(
        d_two_part.astype(jnp.bfloat16), "tensor", scatter_dimension=0, tiled=True
    ).astype(jnp.float32)
    d_middle_norm, mlp_terms = norm_back(middle, mlp_gain, d_norm_two)
    d_middle = out_cot.astype(jnp.float32) + d_middle_norm
    d_middle_all = lax.all_gather(d_middle.astype(jnp.bfloat16), "tensor", axis=0, tiled=True)
    grad_out = rows_first(attn_low, d_middle_all)
    d_mixed = rows_last(d_middle_all, back_out).astype(jnp.bfloat16)
    delta_rows = jnp.sum(
        (d_mixed.astype(jnp.float32) * attn_float).reshape(
            span, kv_heads, sharing_count, HEAD_SIZE
        ),
        axis=-1,
    )
    delta_blocks = delta_rows.reshape(block_count, block_length, kv_heads, sharing_count).transpose(
        0, 2, 3, 1
    )
    d_mixed_blocks = d_mixed.reshape(block_count, block_length, kv_heads, sharing_count, HEAD_SIZE)

    def attend_backward(use_prev):
        begin = 0 if use_prev else span
        dk_total = jnp.zeros((2 * span, kv_heads, HEAD_SIZE), jnp.float32)
        dv_total = jnp.zeros((2 * span, kv_heads, HEAD_SIZE), jnp.float32)
        dq_parts = []
        for index in range(block_count):
            finish = span + (index + 1) * block_length
            query_part = query_tiles[index]
            d_part = d_mixed_blocks[index]
            keys_here = all_keys[begin:finish]
            scores = block_scores(
                query_part,
                segment_blocks[index],
                position_blocks[index],
                keys_here,
                key_segment[begin:finish],
                key_position[begin:finish],
                scaling,
            )
            probability = jnp.exp(scores - log_totals[index][..., None])
            dv_piece = jnp.einsum(
                "hgqk,qhgd->khd",
                probability.astype(jnp.bfloat16),
                d_part,
                preferred_element_type=jnp.float32,
            )
            dv_total = dv_total.at[begin:finish].add(dv_piece)
            d_probs = jnp.einsum(
                "qhgd,khd->hgqk",
                d_part,
                all_values[begin:finish],
                preferred_element_type=jnp.float32,
            )
            d_scores = (probability * (d_probs - delta_blocks[index][..., None])).astype(
                jnp.bfloat16
            )
            dq_parts.append(
                jnp.einsum(
                    "hgqk,khd->qhgd", d_scores, keys_here, preferred_element_type=jnp.float32
                )
                * scaling
            )
            dk_piece = (
                jnp.einsum(
                    "hgqk,qhgd->khd", d_scores, query_part, preferred_element_type=jnp.float32
                )
                * scaling
            )
            dk_total = dk_total.at[begin:finish].add(dk_piece)
        return (dk_total, dv_total, jnp.concatenate(dq_parts, axis=0))

    dk_all, dv_all, dq_rows = lax.cond(
        ctx_index > 0, partial(attend_backward, True), partial(attend_backward, False)
    )
    dk_back, dv_back = (
        from_behind(dk_all[:span].astype(jnp.bfloat16), "ctx", -1).astype(jnp.float32),
        from_behind(dv_all[:span].astype(jnp.bfloat16), "ctx", -1).astype(jnp.float32),
    )
    d_keys = dk_all[span:] + dk_back
    d_values = dv_all[span:] + dv_back
    d_queries = dq_rows.reshape(span, q_heads, HEAD_SIZE)
    dq_linear, query_terms = norm_back(
        q_linear, query_gain, rotate_back(d_queries, cosine_table, sine_table)
    )
    dk_linear, key_terms = norm_back(
        key_linear, key_gain, rotate_back(d_keys, cosine_table, sine_table)
    )
    dq_low = dq_linear.reshape(span, q_heads * HEAD_SIZE).astype(jnp.bfloat16)
    dk_low = dk_linear.reshape(span, kv_heads * HEAD_SIZE).astype(jnp.bfloat16)
    dv_low = d_values.reshape(span, kv_heads * HEAD_SIZE).astype(jnp.bfloat16)
    grad_query = rows_first(norm_one_all, dq_low)
    grad_key = rows_first(norm_one_all, dk_low)
    grad_value = rows_first(norm_one_all, dv_low)
    d_norm_part = (
        rows_last(dq_low, back_query) + rows_last(dk_low, back_key) + rows_last(dv_low, back_value)
    )
    d_norm_one = lax.psum_scatter(
        d_norm_part.astype(jnp.bfloat16), "tensor", scatter_dimension=0, tiled=True
    ).astype(jnp.float32)
    d_rows_norm, attn_terms = norm_back(rows_in, attn_gain, d_norm_one)
    d_tokens = (d_middle + d_rows_norm).astype(jnp.bfloat16)
    gain_totals = lax.psum(
        (
            jnp.sum(attn_terms, axis=0),
            jnp.sum(mlp_terms, axis=0),
            jnp.sum(query_terms, axis=(0, 1)),
            jnp.sum(key_terms, axis=(0, 1)),
        ),
        "tensor",
    )
    shards = (
        lax.psum_scatter(
            grad_query.astype(jnp.bfloat16), ("dp", "ctx"), scatter_dimension=0, tiled=True
        ).astype(jnp.float32),
        lax.psum_scatter(
            grad_key.astype(jnp.bfloat16), ("dp", "ctx"), scatter_dimension=0, tiled=True
        ).astype(jnp.float32),
        lax.psum_scatter(
            grad_value.astype(jnp.bfloat16), ("dp", "ctx"), scatter_dimension=0, tiled=True
        ).astype(jnp.float32),
        lax.psum_scatter(
            grad_out.astype(jnp.bfloat16), ("dp", "ctx"), scatter_dimension=1, tiled=True
        ).astype(jnp.float32),
        lax.psum_scatter(
            grad_gate.astype(jnp.bfloat16), ("dp", "ctx"), scatter_dimension=0, tiled=True
        ).astype(jnp.float32),
        lax.psum_scatter(
            grad_up.astype(jnp.bfloat16), ("dp", "ctx"), scatter_dimension=0, tiled=True
        ).astype(jnp.float32),
        lax.psum_scatter(
            grad_down.astype(jnp.bfloat16), ("dp", "ctx"), scatter_dimension=1, tiled=True
        ).astype(jnp.float32),
        lax.psum_scatter(
            gain_totals[0].astype(jnp.bfloat16), ("dp", "ctx"), scatter_dimension=0, tiled=True
        ).astype(jnp.float32),
        lax.psum_scatter(
            gain_totals[1].astype(jnp.bfloat16), ("dp", "ctx"), scatter_dimension=0, tiled=True
        ).astype(jnp.float32),
        lax.psum_scatter(
            gain_totals[2].astype(jnp.bfloat16), ("dp", "ctx"), scatter_dimension=0, tiled=True
        ).astype(jnp.float32),
        lax.psum_scatter(
            gain_totals[3].astype(jnp.bfloat16), ("dp", "ctx"), scatter_dimension=0, tiled=True
        ).astype(jnp.float32),
    )
    return (
        layer_out,
        d_tokens,
        shards[0],
        shards[1],
        shards[2],
        shards[3],
        shards[4],
        shards[5],
        shards[6],
        shards[7],
        shards[8],
        shards[9],
        shards[10],
    )


def solution(mesh):
    in_specs = (
        P(("dp", "ctx", "tensor"), None),
        P("dp"),
        P(("dp", "ctx"), "tensor"),
        P(("dp", "ctx"), "tensor"),
        P(("dp", "ctx"), "tensor"),
        P("tensor", ("dp", "ctx")),
        P(("dp", "ctx"), "tensor"),
        P(("dp", "ctx"), "tensor"),
        P("tensor", ("dp", "ctx")),
        P(("dp", "ctx")),
        P(("dp", "ctx")),
        P(("dp", "ctx")),
        P(("dp", "ctx")),
        P(("dp", "ctx", "tensor"), None),
    )
    out_specs = (
        P(("dp", "ctx", "tensor"), None),
        P(("dp", "ctx", "tensor"), None),
        P(("dp", "ctx"), "tensor"),
        P(("dp", "ctx"), "tensor"),
        P(("dp", "ctx"), "tensor"),
        P("tensor", ("dp", "ctx")),
        P(("dp", "ctx"), "tensor"),
        P(("dp", "ctx"), "tensor"),
        P("tensor", ("dp", "ctx")),
        P(("dp", "ctx")),
        P(("dp", "ctx")),
        P(("dp", "ctx")),
        P(("dp", "ctx")),
    )
    return jax.shard_map(
        per_device, mesh=mesh, in_specs=in_specs, out_specs=out_specs, check_vma=False
    )
```

profile of v0, /device:TPU:0, one launch (start us, length us, event | category | flops | bytes accessed | tf_op | source)
XLA Modules:
  0.0 1500.5 jit_solution(16292450457754407861)
XLA Ops:
  9.4 22.3 %all-gather = bf16[8,1,128]{2,1,0:T(2,128)(2,1)S(1)} all-gather(bf16[1,1,128]{2,1,0:T(2,128)(2,1)} %bitcast.1148), channel_id=1, replica_groups=mesh['dp'=4,'ctx'=2,'tensor'=4] {'dp','ctx'}, dimensions={0}, use_global_device_ids=true | all-gather | bytes 2304 | tf_op jit(solution)/shard_map/all_gather | solution.py:113
  38.2 17.1 %all-reduce.13 = (bf16[128]{0:T(256)(128)(2,1)S(1)}, bf16[128]{0:T(256)(128)(2,1)S(1)}) all-reduce(bf16[128]{0:T(256)(128)(2,1)S(1)} %dynamic-update-slice.90, bf16[128]{0:T(256)(128)(2,1)S(1)} %dynamic-update-slice.91), channel_id=1, replica_groups=mesh['dp'=4,'ctx'=2,'tensor'=4] {'dp','ctx'}, use_global_device_ids=true, to_apply=%add.5 | all-reduce | flops 256 | bytes 1024
  56.2 34.2 %all_gather.54 = bf16[1024,256]{1,0:T(8,128)(2,1)} all-gather(bf16[128,256]{1,0:T(8,128)(2,1)S(1)} %copy-done.79), channel_id=1, replica_groups=mesh['dp'=4,'ctx'=2,'tensor'=4] {'dp','ctx'}, dimensions={0}, use_global_device_ids=true | all-gather | bytes 589824 | tf_op jit(solution)/shard_map/all_gather | solution.py:107
  90.4 33.4 %all_gather.58 = bf16[1024,256]{1,0:T(8,128)(2,1)} all-gather(bf16[128,256]{1,0:T(8,128)(2,1)S(1)} %copy-done.80), channel_id=1, replica_groups=mesh['dp'=4,'ctx'=2,'tensor'=4] {'dp','ctx'}, dimensions={0}, use_global_device_ids=true | all-gather | bytes 589824 | tf_op jit(solution)/shard_map/all_gather | solution.py:108
  196.4 84.4 %conditional.4 = (f32[4,2,2,512]{3,2,1,0:T(2,128)S(1)}, f32[2048,512]{0,1:T(8,128)}) conditional(s32[]{:T(128)} %convert_element_type.344, (s32[4,512]{1,0:T(4,128)S(1)}, s32[4096]{0:T(1024)S(1)}, s32[4096]{0:T(1024)S(1)}, s32[4,512]{1,0:T(4,128)S(1)}, bf16[2048,2,128]{0,2,1:T(8,128)(2,1)S(1)}, ...), branch_computations={%region_5.14_spmd.clone, %region_14.23_spmd.clone} | conditional | flops 14309408768 | bytes 473514304
  249.3 9.5 fusion.247
  288.4 131.5 %all-gather.1 = bf16[8,1,128]{2,1,0:T(2,128)(2,1)S(1)} all-gather(bf16[1,1,128]{2,1,0:T(2,128)(2,1)S(1)} %bitcast.1149), channel_id=1, replica_groups=mesh['dp'=4,'ctx'=2,'tensor'=4] {'dp','ctx'}, dimensions={0}, use_global_device_ids=true | all-gather | bytes 2304 | tf_op jit(solution)/shard_map/all_gather | solution.py:114
  419.9 24.9 %reduce-scatter.16.cloned.1.call-done = bf16[512,1024]{1,0:T(8,128)(2,1)} async-done(((bf16[2048,1024]{1,0:T(8,128)(2,1)}), bf16[512,1024]{1,0:T(8,128)(2,1)}) %reduce-scatter.16.cloned.1.call-update) | async-done | bytes 1048592 | tf_op jit(solution)/shard_map/reduce_scatter | solution.py:208
  451.4 40.0 %all-gather.22.cloned.1.call-done = bf16[1024,768]{1,0:T(8,128)(2,1)} async-done(((bf16[128,768]{1,0:T(8,128)(2,1)}), bf16[1024,768]{1,0:T(8,128)(2,1)}) %all-gather.22.cloned.1.call-update) | async-done | bytes 1572880 | tf_op jit(solution)/shard_map/all_gather | solution.py:111
  491.4 34.8 %all-gather.18.cloned.1.call-done = bf16[2048,1024]{1,0:T(8,128)(2,1)} async-done(((bf16[512,1024]{1,0:T(8,128)(2,1)}), bf16[2048,1024]{1,0:T(8,128)(2,1)}) %all-gather.18.cloned.1.call-update) | async-done | bytes 4194320 | tf_op jit(solution)/shard_map/all_gather | solution.py:213
  526.2 8.8 fusion.364
  535.0 37.8 %all-gather.20.cloned.1.call-done = bf16[1024,768]{1,0:T(8,128)(2,1)} async-done(((bf16[128,768]{1,0:T(8,128)(2,1)}), bf16[1024,768]{1,0:T(8,128)(2,1)}) %all-gather.20.cloned.1.call-update) | async-done | bytes 1572880 | tf_op jit(solution)/shard_map/all_gather | solution.py:110
  572.8 8.7 fusion.363
  581.6 37.6 %all-gather.24.cloned.1.call-done = bf16[768,1024]{1,0:T(8,128)(2,1)} async-done(((bf16[768,128]{1,0:T(8,128)(2,1)}), bf16[768,1024]{1,0:T(8,128)(2,1)}) %all-gather.24.cloned.1.call-update) | async-done | bytes 1572880 | tf_op jit(solution)/shard_map/all_gather | solution.py:112
  619.2 34.3 %all-gather.26.cloned.1.call-done = bf16[2048,1024]{1,0:T(8,128)(2,1)} async-done(((bf16[512,1024]{1,0:T(8,128)(2,1)}), bf16[2048,1024]{1,0:T(8,128)(2,1)}) %all-gather.26.cloned.1.call-update) | async-done | bytes 4194320 | tf_op jit(solution)/shard_map/all_gather | solution.py:235
  653.6 11.9 multiply_convert_fusion
  674.4 44.8 %reduce-scatter.20.cloned.1.call-done = bf16[512,1024]{1,0:T(8,128)(2,1)} async-done(((bf16[2048,1024]{1,0:T(8,128)(2,1)}), bf16[512,1024]{1,0:T(8,128)(2,1)}) %reduce-scatter.20.cloned.1.call-update) | async-done | bytes 1048592 | tf_op jit(solution)/shard_map/reduce_scatter | solution.py:246
  750.8 9.1 all-gather.28.cloned.1.call-done
  772.0 148.6 %conditional.3 = (f32[2048,512]{0,1:T(8,128)}, f32[2048,4,128]{2,0,1:T(8,128)}, f32[4096,2,128]{0,2,1:T(8,128)}, f32[2048,2,128]{0,2,1:T(8,128)}, f32[4096,2,128]{0,2,1:T(8,128)}, /*index=5*/f32[2048,2,128]{0,2,1:T(8,128)}) conditional(s32[]{:T(128)} %convert_element_type.344, (s32[4,512]{1,0:T(4,128)S(1)}, s32[4096]{0:T(1024)S(1)}, ...), branch_computations={%region_29.30_spmd.clone, %region_30.31_spmd.clone} | conditional | flops 35202793472 | bytes 736706880 | solution.py:316
  817.4 9.6 fusion.35
  850.7 12.7 fusion.52
  863.5 10.3 fusion.1
  939.9 9.0 multiply_reduce_fusion
  956.6 176.3 %collective-permute-done.3 = bf16[2048,2,128]{0,2,1:T(8,128)(2,1)} collective-permute-done((bf16[2048,2,128]{0,2,1:T(8,128)(2,1)}, bf16[2048,2,128]{0,2,1:T(8,128)(2,1)}, u32[]{:S(2)}, u32[]{:S(2)}) %collective-permute-start.3) | collective-permute-done | bytes 1048608 | tf_op jit(solution)/shard_map/ppermute | solution.py:18
  1138.2 18.1 %collective-permute-done.2 = bf16[2048,2,128]{0,2,1:T(8,128)(2,1)S(1)} collective-permute-done((bf16[2048,2,128]{0,2,1:T(8,128)(2,1)}, bf16[2048,2,128]{0,2,1:T(8,128)(2,1)S(1)}, u32[]{:S(2)}, u32[]{:S(2)}) %collective-permute-start.2) | collective-permute-done | bytes 1048608 | tf_op jit(solution)/shard_map/ppermute | solution.py:18
  1206.8 58.4 %reduce-scatter.28.cloned.1.call-done = bf16[128,256]{1,0:T(8,128)(2,1)} async-done(((bf16[1024,256]{1,0:T(8,128)(2,1)}), bf16[128,256]{1,0:T(8,128)(2,1)}) %reduce-scatter.28.cloned.1.call-update) | async-done | bytes 65552 | tf_op jit(solution)/shard_map/reduce_scatter | solution.py:362
  1266.7 63.0 %reduce-scatter.26.cloned.1.call-done = bf16[128,256]{1,0:T(8,128)(2,1)} async-done(((bf16[1024,256]{1,0:T(8,128)(2,1)}), bf16[128,256]{1,0:T(8,128)(2,1)}) %reduce-scatter.26.cloned.1.call-update) | async-done | bytes 65552 | tf_op jit(solution)/shard_map/reduce_scatter | solution.py:359
  1331.2 64.8 %reduce-scatter.24.cloned.1.call-done = bf16[128,512]{1,0:T(8,128)(2,1)} async-done(((bf16[1024,512]{1,0:T(8,128)(2,1)}), bf16[128,512]{1,0:T(8,128)(2,1)}) %reduce-scatter.24.cloned.1.call-update) | async-done | bytes 131088 | tf_op jit(solution)/shard_map/reduce_scatter | solution.py:356
  1397.7 44.6 %reduce-scatter.22.cloned.1.call-done = bf16[512,1024]{1,0:T(8,128)(2,1)} async-done(((bf16[2048,1024]{1,0:T(8,128)(2,1)}), bf16[512,1024]{1,0:T(8,128)(2,1)}) %reduce-scatter.22.cloned.1.call-update) | async-done | bytes 1048592 | tf_op jit(solution)/shard_map/reduce_scatter | solution.py:341
  1444.4 10.2 all-reduce.11
  1454.6 21.7 %all-reduce.12 = (bf16[1024]{0:T(1024)(128)(2,1)S(1)}, bf16[1024]{0:T(1024)(128)(2,1)S(1)}, bf16[128]{0:T(256)(128)(2,1)S(1)}, bf16[128]{0:T(256)(128)(2,1)S(1)}) all-reduce(bf16[1024]{0:T(1024)(128)(2,1)S(1)} %get-tuple-element.724, ...), channel_id=13, replica_groups=mesh['dp'=4,'ctx'=2,'tensor'=4] {'dp','ctx'}, use_global_device_ids=true, to_apply=%region_44.45.clone | all-reduce | flops 2304 | bytes 9216
  1478.6 10.6 reduce-scatter.18.cloned.1.call-done
  (416 shorter events, 402.8 us)
Async XLA Ops:
  7.2 127.6 %all-gather.12.cloned.1.call-start = ((), (), s32[]{:S(2)}) async-start(), calls=%async_computation.11 | async-start | bytes 5242880 | tf_op jit(solution)/shard_map/all_gather | solution.py:136
  34.9 116.6 %all-gather.14.cloned.1.call-start = ((), (), s32[]{:S(2)}) async-start(), calls=%async_computation.12 | async-start | bytes 1179648 | tf_op jit(solution)/shard_map/all_gather | solution.py:106
  35.6 245.2 %all-gather.16.cloned.1.call-start = ((), (), s32[]{:S(2)}) async-start(), calls=%async_computation.13 | async-start | bytes 1179648 | tf_op jit(solution)/shard_map/all_gather | solution.py:109
  36.4 408.5 %reduce-scatter.16.cloned.1.call-start = ((), (), s32[]{:S(2)}) async-start(), calls=%async_computation.14 | async-start | bytes 5242880 | tf_op jit(solution)/shard_map/reduce_scatter | solution.py:208
  139.8 51.2 %collective-permute-start.1 = (bf16[2048,2,128]{2,0,1:T(8,128)(2,1)}, bf16[2048,2,128]{2,0,1:T(8,128)(2,1)}, u32[]{:S(2)}, u32[]{:S(2)}) collective-permute-start(bf16[2048,2,128]{2,0,1:T(8,128)(2,1)} %copy.232), channel_id=1, source_target_pairs={{0,4},{1,5},{2,6},{3,7},{8,12},{9,13},{10,14},{11,15},{16,20},{17,... | collective-permute-start | bytes 3145736 | tf_op jit(solution)/shard_map/ppermute | solution.py:18
  149.2 44.5 %collective-permute-start = (bf16[2048,2,128]{0,2,1:T(8,128)(2,1)S(1)}, bf16[2048,2,128]{0,2,1:T(8,128)(2,1)}, u32[]{:S(2)}, u32[]{:S(2)}) collective-permute-start(bf16[2048,2,128]{0,2,1:T(8,128)(2,1)S(1)} %fusion.344), channel_id=1, source_target_pairs={{0,4},{1,5},{2,6},{3,7},{8,12},{9,13},{10,14},{11,15},{16,20},{17,... | collective-permute-start | bytes 3145736 | tf_op jit(solution)/shard_map/ppermute | solution.py:18
  287.8 203.6 %all-gather.22.cloned.1.call-start = ((), (), s32[]{:S(2)}) async-start(), calls=%async_computation.17 | async-start | bytes 1769472 | tf_op jit(solution)/shard_map/all_gather | solution.py:111
  288.4 237.8 %all-gather.18.cloned.1.call-start = ((), (), s32[]{:S(2)}) async-start(), calls=%async_computation.15 | async-start | bytes 5242880 | tf_op jit(solution)/shard_map/all_gather | solution.py:213
  419.9 301.9 %copy-start.74 = (f32[8,1,128]{2,1,0:T(1,128)}, f32[8,1,128]{2,1,0:T(1,128)S(1)}, u32[]{:S(2)}) copy-start(f32[8,1,128]{2,1,0:T(1,128)S(1)} %convert_element_type.421) | copy-start | bytes 12292
  449.2 123.7 %all-gather.20.cloned.1.call-start = ((), (), s32[]{:S(2)}) async-start(), calls=%async_computation.16 | async-start | bytes 1769472 | tf_op jit(solution)/shard_map/all_gather | solution.py:110
  449.9 169.3 %all-gather.24.cloned.1.call-start = ((), (), s32[]{:S(2)}) async-start(), calls=%async_computation.18 | async-start | bytes 1769472 | tf_op jit(solution)/shard_map/all_gather | solution.py:112
  450.7 202.9 %all-gather.26.cloned.1.call-start = ((), (), s32[]{:S(2)}) async-start(), calls=%async_computation.20 | async-start | bytes 5242880 | tf_op jit(solution)/shard_map/all_gather | solution.py:235
  451.4 267.8 %reduce-scatter.20.cloned.1.call-start = ((), (), s32[]{:S(2)}) async-start(), calls=%async_computation.21 | async-start | bytes 5242880 | tf_op jit(solution)/shard_map/reduce_scatter | solution.py:246
  674.3 85.6 %all-gather.28.cloned.1.call-start = ((), (), s32[]{:S(2)}) async-start(), calls=%async_computation.22 | async-start | bytes 5242880 | tf_op jit(solution)/shard_map/all_gather | solution.py:251
  725.3 474.5 %reduce-scatter.36.cloned.1.call-start = ((), (), s32[]{:S(2)}) async-start(), calls=%async_computation.30 | async-start | bytes 1769472
  734.0 467.6 %reduce-scatter.32.cloned.1.call-start = ((), (), s32[]{:S(2)}) async-start(), calls=%async_computation.28 | async-start | bytes 1769472 | tf_op jit(solution)/shard_map/reduce_scatter | solution.py:371
  742.1 461.2 %reduce-scatter.30.cloned.1.call-start = ((), (), s32[]{:S(2)}) async-start(), calls=%async_computation.27 | async-start | bytes 1769472 | tf_op jit(solution)/shard_map/reduce_scatter | solution.py:368
  750.8 454.3 %reduce-scatter.34.cloned.1.call-start = ((), (), s32[]{:S(2)}) async-start(), calls=%async_computation.29 | async-start | bytes 1179648
  926.2 206.7 %collective-permute-start.3 = (bf16[2048,2,128]{0,2,1:T(8,128)(2,1)}, bf16[2048,2,128]{0,2,1:T(8,128)(2,1)}, u32[]{:S(2)}, u32[]{:S(2)}) collective-permute-start(bf16[2048,2,128]{0,2,1:T(8,128)(2,1)} %slice.1664), channel_id=1, source_target_pairs={{4,0},{5,1},{6,2},{7,3},{12,8},{13,9},{14,10},{15,11},{20,16},{21,... | collective-permute-start | bytes 3145736 | tf_op jit(solution)/shard_map/ppermute | solution.py:18
  927.5 228.9 %collective-permute-start.2 = (bf16[2048,2,128]{0,2,1:T(8,128)(2,1)}, bf16[2048,2,128]{0,2,1:T(8,128)(2,1)S(1)}, u32[]{:S(2)}, u32[]{:S(2)}) collective-permute-start(bf16[2048,2,128]{0,2,1:T(8,128)(2,1)} %slice.1665), channel_id=1, source_target_pairs={{4,0},{5,1},{6,2},{7,3},{12,8},{13,9},{14,10},{15,11},{20,16},{21,... | collective-permute-start | bytes 3145736 | tf_op jit(solution)/shard_map/ppermute | solution.py:18
  956.6 308.6 %reduce-scatter.28.cloned.1.call-start = ((), (), s32[]{:S(2)}) async-start(), calls=%async_computation.26 | async-start | bytes 589824 | tf_op jit(solution)/shard_map/reduce_scatter | solution.py:362
  1161.6 168.2 %reduce-scatter.26.cloned.1.call-start = ((), (), s32[]{:S(2)}) async-start(), calls=%async_computation.25 | async-start | bytes 589824 | tf_op jit(solution)/shard_map/reduce_scatter | solution.py:359
  1170.1 226.0 %reduce-scatter.24.cloned.1.call-start = ((), (), s32[]{:S(2)}) async-start(), calls=%async_computation.24 | async-start | bytes 1179648 | tf_op jit(solution)/shard_map/reduce_scatter | solution.py:356
  1180.8 261.5 %reduce-scatter.22.cloned.1.call-start = ((), (), s32[]{:S(2)}) async-start(), calls=%async_computation.23 | async-start | bytes 5242880 | tf_op jit(solution)/shard_map/reduce_scatter | solution.py:341
  1189.8 299.5 %reduce-scatter.18.cloned.1.call-start = ((), (), s32[]{:S(2)}) async-start(), calls=%async_computation.19 | async-start | bytes 5242880 | tf_op jit(solution)/shard_map/reduce_scatter | solution.py:217
  1198.1 291.1 %copy-start.16 = (bf16[512,1024]{1,0:T(8,128)(2,1)S(1)}, bf16[512,1024]{1,0:T(8,128)(2,1)}, u32[]{:S(2)}) copy-start(bf16[512,1024]{1,0:T(8,128)(2,1)} %reduce-scatter.16.cloned.1.call-done) | copy-start | bytes 3145732
  1198.1 291.1 %copy-start.29 = (bf16[512,1024]{1,0:T(8,128)(2,1)S(1)}, bf16[512,1024]{1,0:T(8,128)(2,1)}, u32[]{:S(2)}) copy-start(bf16[512,1024]{1,0:T(8,128)(2,1)} %param.67) | copy-start | bytes 3145732
  1198.1 291.1 %copy-start.75 = (f32[8,1,128]{2,1,0:T(1,128)S(1)}, f32[8,1,128]{2,1,0:T(1,128)}, u32[]{:S(2)}) copy-start(f32[8,1,128]{2,1,0:T(1,128)} %copy-done.74) | copy-start | bytes 12292
  1198.1 291.1 %copy-start.82 = (f32[512]{0:T(512)S(1)}, f32[512]{0:T(512)}, u32[]{:S(2)}) copy-start(f32[512]{0:T(512)} %copy-done.81) | copy-start | bytes 6148
  1198.1 291.1 %copy-start.87 = (f32[512]{0:T(512)S(1)}, f32[512]{0:T(512)}, u32[]{:S(2)}) copy-start(f32[512]{0:T(512)} %copy-done.86) | copy-start | bytes 6148
  1198.2 291.1 %copy-start.89 = (f32[512]{0:T(512)S(1)}, f32[512]{0:T(512)}, u32[]{:S(2)}) copy-start(f32[512]{0:T(512)} %copy-done.88) | copy-start | bytes 6148
  1198.2 291.1 %copy-start.97 = (f32[512]{0:T(512)S(1)}, f32[512]{0:T(512)}, u32[]{:S(2)}) copy-start(f32[512]{0:T(512)} %get-tuple-element.846) | copy-start | bytes 6148
  (84 other events, 2816.9 us)
Sparse Core Ops, SparseCore 0:
  35.0 31.7 all-gather.11
  68.9 42.9 all-gather.13
  113.9 38.3 all-gather.15
  287.9 156.9 reduce-scatter.15
  447.1 44.2 all-gather.21
  492.9 33.2 all-gather.17
  528.6 44.1 all-gather.19
  575.1 44.0 all-gather.23
  620.9 32.6 all-gather.25
  674.4 44.6 reduce-scatter.19
  725.4 34.4 all-gather.27
  763.2 64.7 reduce-scatter.35
  831.8 63.7 reduce-scatter.31
  898.9 63.7 reduce-scatter.29
  966.3 234.6 reduce-scatter.33
  1204.2 61.0 reduce-scatter.27
  1268.8 60.9 reduce-scatter.25
  1333.6 62.4 reduce-scatter.23
  1398.8 43.5 reduce-scatter.21
  1444.7 44.4 reduce-scatter.17
where the time goes:
time: 1510 us; the launch traced here: 1500 us
  waiting for transfers between devices  704 us (47%)
  blocking collectives  270 us (18%)
  matrix products  239 us (16%)
  other arithmetic  122 us (8%)
  local copies, waits for them, and re-layouts  110 us (7%)
  loops' own time  29.4 us (2%)
  between operations  17.9 us (1%)
    ppermute x4, waiting for transfers between devices, from_behind(): return lax.ppermute(shard, axis, pairs)  194 us
    all_gather x1, blocking collectives, per_device(): lax.all_gather(gain_mlp, ('dp', 'ctx'), axis=0, tiled=True)  132 us
    reduce_scatter x1, waiting for transfers between devices, per_device(): lax.psum_scatter(grad_query.astype(jnp.bfloat16), ('dp', 'ctx'), scatter_...  64.8 us
    reduce_scatter x1, waiting for transfers between devices, per_device(): lax.psum_scatter(grad_key.astype(jnp.bfloat16), ('dp', 'ctx'), scatter_di...  63 us
    reduce_scatter x1, waiting for transfers between devices, per_device(): lax.psum_scatter(grad_value.astype(jnp.bfloat16), ('dp', 'ctx'), scatter_...  58.4 us
    reduce_scatter x1, waiting for transfers between devices, per_device(): lax.psum_scatter(d_two_part.astype(jnp.bfloat16), 'tensor', scatter_dimen...  44.8 us
    reduce_scatter x1, waiting for transfers between devices, per_device(): lax.psum_scatter(d_norm_part.astype(jnp.bfloat16), 'tensor', scatter_dime...  44.6 us
    all_gather x1, waiting for transfers between devices, per_device(): lax.all_gather(w_up, ('dp', 'ctx'), axis=0, tiled=True)  40 us
  transfers between devices with their start and end apart: 24, of which 15 were waited for; matrix products, arithmetic and copies ran while one was open for 27% of the time, Pallas kernels for 0%

commit v1 on v0

v1 whole, which is shorter than its diff:
```python
import functools
import math

import jax
import jax.numpy as jnp
from jax import lax
from jax.experimental import pallas as pl
from jax.experimental.pallas import tpu as pltpu
from jax.sharding import PartitionSpec as P

HEAD_SIZE = 128


EPS = 1e-06
THETA = 1000000.0


def from_behind(shard, axis, by):
    length = lax.axis_size(axis)
    pairs = [(i, i + by) for i in range(length) if 0 <= i + by < length]
    return lax.ppermute(shard, axis, pairs)


def norm_rows(field, gain):
    return field * lax.rsqrt(jnp.mean(field * field, axis=-1, keepdims=True) + EPS) * gain


def norm_back(field, gain, incoming):
    inverse = lax.rsqrt(jnp.mean(field * field, axis=-1, keepdims=True) + EPS)
    scaled = incoming * gain
    d_field = inverse * scaled - field * (inverse * inverse * inverse) * jnp.mean(
        scaled * field, axis=-1, keepdims=True
    )
    return (d_field, incoming * field * inverse)


SCALE = HEAD_SIZE ** (-0.5)
SCALE_LOG2 = SCALE * math.log2(math.e)
D = HEAD_SIZE
ROWS_TILE = 256
BQ = 256
BK = 512


def rotary_own(segment, ctx_index, span):
    length_total = segment.shape[0]
    positions = jnp.arange(length_total, dtype=jnp.int32)
    begins = jnp.concatenate([jnp.ones((1,), dtype=jnp.bool_), segment[1:] != segment[:-1]])
    starts = lax.cummax(jnp.where(begins, positions, jnp.zeros_like(positions)), axis=0)
    starts = lax.dynamic_slice_in_dim(starts, ctx_index * span, span, 0)
    mine = ctx_index * span + jnp.arange(span, dtype=jnp.int32)
    offset = (mine - starts).astype(jnp.float32)
    frequency = THETA ** (-2.0 * jnp.arange(D // 2, dtype=jnp.float32) / D)
    angles = offset[:, None] * frequency[None, :]
    cosine = jnp.cos(angles)
    sine = jnp.sin(angles)
    return (
        jnp.concatenate([cosine, cosine], axis=-1),
        jnp.concatenate([-sine, sine], axis=-1),
        starts - (ctx_index - 1) * span,
    )


def head_back(lin, gain, e):
    inverse = lax.rsqrt(jnp.mean(lin * lin, axis=-1, keepdims=True) + EPS)
    scaled = e * gain
    d_lin = inverse * scaled - lin * (inverse * inverse * inverse) * jnp.mean(
        scaled * lin, axis=-1, keepdims=True
    )
    return d_lin, e * lin * inverse


def turn_back(z, cosine, sine):
    return z * cosine - pltpu.roll(z, D // 2, 1) * sine


def qkv_kernel(
    q_heads, kv_heads, x_ref, gain_ref, w_ref, cos_ref, sin_ref, qg_ref, kg_ref,
    n_ref, lin_ref, q_ref, kv_ref,
):
    normed = norm_rows(x_ref[...].astype(jnp.float32), gain_ref[...]).astype(jnp.bfloat16)
    n_ref[...] = normed
    lin = jnp.dot(normed, w_ref[...], preferred_element_type=jnp.float32)
    both = q_heads + kv_heads
    lin_ref[...] = lin[:, : both * D]
    cosine, sine = cos_ref[...], sin_ref[...]
    for h in range(both):
        gain = qg_ref[...] if h < q_heads else kg_ref[...]
        y = norm_rows(lin[:, h * D : (h + 1) * D], gain)
        y = (y * cosine + pltpu.roll(y, D // 2, 1) * sine).astype(jnp.bfloat16)
        if h < q_heads:
            q_ref[:, h * D : (h + 1) * D] = y
        else:
            kv_ref[:, (h - q_heads) * D : (h - q_heads + 1) * D] = y
    kv_ref[:, kv_heads * D :] = lin[:, both * D :].astype(jnp.bfloat16)


def qkv_call(x, gain, w, cosine, sine, query_gain, key_gain, q_heads, kv_heads):
    rows, width = x.shape
    row = lambda n: pl.BlockSpec((ROWS_TILE, n), lambda i: (i, 0))
    one = lambda s: pl.BlockSpec(s, lambda i: (0, 0))
    both = q_heads + kv_heads
    return pl.pallas_call(
        functools.partial(qkv_kernel, q_heads, kv_heads),
        grid=(rows // ROWS_TILE,),
        in_specs=[row(width), one((1, width)), one(w.shape), row(D), row(D), one((1, D)), one((1, D))],
        out_specs=[row(width), row(both * D), row(q_heads * D), row(2 * kv_heads * D)],
        out_shape=[
            jax.ShapeDtypeStruct((rows, width), jnp.bfloat16),
            jax.ShapeDtypeStruct((rows, both * D), jnp.float32),
            jax.ShapeDtypeStruct((rows, q_heads * D), jnp.bfloat16),
            jax.ShapeDtypeStruct((rows, 2 * kv_heads * D), jnp.bfloat16),
        ],
        compiler_params=pltpu.CompilerParams(vmem_limit_bytes=40 * 2**20),
        cost_estimate=pl.CostEstimate(
            flops=2 * rows * width * w.shape[1], bytes_accessed=rows * 12000, transcendentals=0
        ),
        name="qkv_forward",
    )(x, gain, w, cosine, sine, query_gain, key_gain)


def stack_heads(block, share):
    return jnp.concatenate([block[:, g * D : (g + 1) * D] for g in range(share)], axis=0)


def forward_kernel(
    span, share, lo_ref, late_ref, q_ref, k_ref, v_ref, st_ref, o_ref, li_ref, vext, acc
):
    i = pl.program_id(1)

    @pl.when(i == 0)
    def _():
        vext[:, :D] = v_ref[...]
        vext[:, D:] = jnp.ones_like(v_ref)

    q2 = stack_heads(q_ref[...], share)
    acc[...] = jnp.zeros_like(acc)
    first = span + i * BQ

    def step(kb, masked):
        ks = pl.multiple_of(kb * BK, BK)
        s = lax.dot_general(
            q2, k_ref[pl.ds(ks, BK), :], (((1,), (1,)), ((), ())),
            preferred_element_type=jnp.float32,
        )
        p = jnp.exp2(s * SCALE_LOG2)
        if masked:
            rows = first + lax.broadcasted_iota(jnp.int32, (BQ, BK), 0)
            cols = ks + lax.broadcasted_iota(jnp.int32, (BQ, BK), 1)
            keep = (cols <= rows) & (cols >= st_ref[:, :1])
            keep = jnp.where(keep, 1.0, 0.0)
            p = jnp.where(jnp.concatenate([keep] * share, axis=0) > 0.5, p, 0.0)
        acc[...] += jnp.dot(
            p.astype(jnp.bfloat16), vext[pl.ds(ks, BK), :], preferred_element_type=jnp.float32
        )

    def body(kb, carry):
        full = (kb * BK >= late_ref[i]) & ((kb + 1) * BK - 1 <= first)
        pl.when(full)(lambda: step(kb, False))
        pl.when(jnp.logical_not(full))(lambda: step(kb, True))
        return carry

    lax.fori_loop(lo_ref[i], (first + BQ + BK - 1) // BK, body, 0)
    inverse = 1.0 / acc[:, D:]
    out = (acc[:, :D] * inverse).astype(jnp.bfloat16)
    for g in range(share):
        o_ref[:, g * D : (g + 1) * D] = out[g * BQ : (g + 1) * BQ]
        li_ref[:, g * D : (g + 1) * D] = inverse[g * BQ : (g + 1) * BQ]


def forward_call(lo, late, q, kv_all, start_cols, kv_heads):
    span, q_width = q.shape
    share = q_width // D // kv_heads
    tile = pl.BlockSpec((BQ, share * D), lambda h, i, *_: (i, h))
    return pl.pallas_call(
        functools.partial(forward_kernel, span, share),
        grid_spec=pltpu.PrefetchScalarGridSpec(
            num_scalar_prefetch=2,
            grid=(kv_heads, span // BQ),
            in_specs=[
                tile,
                pl.BlockSpec((2 * span, D), lambda h, i, *_: (0, h)),
                pl.BlockSpec((2 * span, D), lambda h, i, *_: (0, kv_heads + h)),
                pl.BlockSpec((BQ, D), lambda h, i, *_: (i, 0)),
            ],
            out_specs=[tile, tile],
            scratch_shapes=[
                pltpu.VMEM((2 * span, 2 * D), jnp.bfloat16),
                pltpu.VMEM((share * BQ, 2 * D), jnp.float32),
            ],
        ),
        out_shape=[
            jax.ShapeDtypeStruct((span, q_width), jnp.bfloat16),
            jax.ShapeDtypeStruct((span, q_width), jnp.float32),
        ],
        compiler_params=pltpu.CompilerParams(vmem_limit_bytes=40 * 2**20),
        cost_estimate=pl.CostEstimate(
            flops=20 * span * span * q_width, bytes_accessed=20 * span * q_width,
            transcendentals=2 * span * span * q_width // D,
        ),
        name="attention_forward",
    )(lo, late, q, kv_all, kv_all, start_cols)


def backward_kernel(
    span, share, lo_ref, late_ref, q_ref, do_ref, o_ref, li_ref, lin_ref, cos_ref, sin_ref,
    st_ref, gain_ref, k_ref, v_ref, dq_ref, dk_ref, dv_ref, term_ref, dq_acc,
):
    h, i = pl.program_id(0), pl.program_id(1)

    @pl.when(i == 0)
    def _():
        dk_ref[...] = jnp.zeros_like(dk_ref)
        dv_ref[...] = jnp.zeros_like(dv_ref)

    @pl.when((i == 0) & (h == 0))
    def _():
        term_ref[...] = jnp.zeros_like(term_ref)

    q2 = stack_heads(q_ref[...], share)
    do2 = stack_heads(do_ref[...].astype(jnp.float32) * li_ref[...], share).astype(jnp.bfloat16)
    product = do2.astype(jnp.float32) * stack_heads(o_ref[...], share).astype(jnp.float32)
    delta = lax.dot_general(
        jnp.ones((8, D), jnp.float32), product, (((1,), (1,)), ((), ())),
        precision=lax.Precision.HIGHEST, preferred_element_type=jnp.float32,
    )[0:1]
    dq_acc[...] = jnp.zeros_like(dq_acc)
    first = span + i * BQ

    def step(kb, masked):
        ks = pl.multiple_of(kb * BK, BK)
        k = k_ref[pl.ds(ks, BK), :]
        s = lax.dot_general(
            k, q2, (((1,), (1,)), ((), ())), preferred_element_type=jnp.float32
        )
        p = jnp.exp2(s * SCALE_LOG2)
        if masked:
            rows = ks + lax.broadcasted_iota(jnp.int32, (BK, BQ), 0)
            cols = first + lax.broadcasted_iota(jnp.int32, (BK, BQ), 1)
            keep = (rows <= cols) & (rows >= st_ref[0:1, :])
            keep = jnp.where(keep, 1.0, 0.0)
            p = jnp.where(jnp.concatenate([keep] * share, axis=1) > 0.5, p, 0.0)
        dv_ref[pl.ds(ks, BK), :] += jnp.dot(
            p.astype(jnp.bfloat16), do2, preferred_element_type=jnp.float32
        )
        dp = lax.dot_general(
            v_ref[pl.ds(ks, BK), :], do2, (((1,), (1,)), ((), ())),
            preferred_element_type=jnp.float32,
        )
        ds = (p * (dp - delta)).astype(jnp.bfloat16)
        dk_ref[pl.ds(ks, BK), :] += jnp.dot(ds, q2, preferred_element_type=jnp.float32)
        dq_acc[...] += lax.dot_general(
            ds, k, (((0,), (0,)), ((), ())), preferred_element_type=jnp.float32
        )

    def body(kb, carry):
        full = (kb * BK >= late_ref[i]) & ((kb + 1) * BK - 1 <= first)
        pl.when(full)(lambda: step(kb, False))
        pl.when(jnp.logical_not(full))(lambda: step(kb, True))
        return carry

    lax.fori_loop(lo_ref[i], (first + BQ + BK - 1) // BK, body, 0)
    for g in range(share):
        e = turn_back(dq_acc[g * BQ : (g + 1) * BQ] * SCALE, cos_ref[...], sin_ref[...])
        d_lin, terms = head_back(lin_ref[:, g * D : (g + 1) * D], gain_ref[...], e)
        dq_ref[:, g * D : (g + 1) * D] = d_lin.astype(jnp.bfloat16)
        term_ref[0:1, :] += jnp.sum(terms, axis=0, keepdims=True)

    @pl.when(i == pl.num_programs(1) - 1)
    def _():
        dk_ref[...] = dk_ref[...] * SCALE


def backward_call(lo, late, q, d_mixed, mixed, inverse, lin, cosine, sine, start_rows, gain, kv_all, kv_heads):
    span, q_width = q.shape
    share = q_width // D // kv_heads
    tile = pl.BlockSpec((BQ, share * D), lambda h, i, *_: (i, h))
    table = pl.BlockSpec((BQ, D), lambda h, i, *_: (i, 0))
    whole = pl.BlockSpec((2 * span, D), lambda h, i, *_: (0, h))
    return pl.pallas_call(
        functools.partial(backward_kernel, span, share),
        grid_spec=pltpu.PrefetchScalarGridSpec(
            num_scalar_prefetch=2,
            grid=(kv_heads, span // BQ),
            in_specs=[
                tile, tile, tile, tile, tile, table, table,
                pl.BlockSpec((8, BQ), lambda h, i, *_: (0, i)),
                pl.BlockSpec((1, D), lambda h, i, *_: (0, 0)),
                whole,
                pl.BlockSpec((2 * span, D), lambda h, i, *_: (0, kv_heads + h)),
            ],
            out_specs=[tile, whole, whole, pl.BlockSpec((8, D), lambda h, i, *_: (0, 0))],
            scratch_shapes=[pltpu.VMEM((share * BQ, D), jnp.float32)],
        ),
        out_shape=[
            jax.ShapeDtypeStruct((span, q_width), jnp.bfloat16),
            jax.ShapeDtypeStruct((2 * span, kv_heads * D), jnp.float32),
            jax.ShapeDtypeStruct((2 * span, kv_heads * D), jnp.float32),
            jax.ShapeDtypeStruct((8, D), jnp.float32),
        ],
        compiler_params=pltpu.CompilerParams(vmem_limit_bytes=48 * 2**20),
        cost_estimate=pl.CostEstimate(
            flops=50 * span * span * q_width, bytes_accessed=40 * span * q_width,
            transcendentals=2 * span * span * q_width // D,
        ),
        name="attention_backward",
    )(lo, late, q, d_mixed, mixed, inverse, lin, cosine, sine, start_rows, gain, kv_all, kv_all)


def keys_back_kernel(kv_heads, dk_ref, dv_ref, come_ref, lin_ref, cos_ref, sin_ref, gain_ref, out_ref, term_ref):
    @pl.when(pl.program_id(0) == 0)
    def _():
        term_ref[...] = jnp.zeros_like(term_ref)

    come = come_ref[...].astype(jnp.float32)
    d_keys = dk_ref[...] + come[:, : kv_heads * D]
    out_ref[:, kv_heads * D :] = (dv_ref[...] + come[:, kv_heads * D :]).astype(jnp.bfloat16)
    for h in range(kv_heads):
        part = slice(h * D, (h + 1) * D)
        e = turn_back(d_keys[:, part], cos_ref[...], sin_ref[...])
        d_lin, terms = head_back(lin_ref[:, part], gain_ref[...], e)
        out_ref[:, part] = d_lin.astype(jnp.bfloat16)
        term_ref[0:1, :] += jnp.sum(terms, axis=0, keepdims=True)


def keys_back_call(dk_all, dv_all, come, lin, cosine, sine, gain, kv_heads):
    span = come.shape[0]
    tiles = span // ROWS_TILE
    width = kv_heads * D
    skip = (lin.shape[1] - width) // width
    later = pl.BlockSpec((ROWS_TILE, width), lambda i: (tiles + i, 0))
    table = pl.BlockSpec((ROWS_TILE, D), lambda i: (i, 0))
    return pl.pallas_call(
        functools.partial(keys_back_kernel, kv_heads),
        grid=(tiles,),
        in_specs=[
            later, later,
            pl.BlockSpec((ROWS_TILE, 2 * width), lambda i: (i, 0)),
            pl.BlockSpec((ROWS_TILE, width), lambda i: (i, skip)),
            table, table,
            pl.BlockSpec((1, D), lambda i: (0, 0)),
        ],
        out_specs=[
            pl.BlockSpec((ROWS_TILE, 2 * width), lambda i: (i, 0)),
            pl.BlockSpec((8, D), lambda i: (0, 0)),
        ],
        out_shape=[
            jax.ShapeDtypeStruct((span, 2 * width), jnp.bfloat16),
            jax.ShapeDtypeStruct((8, D), jnp.float32),
        ],
        compiler_params=pltpu.CompilerParams(vmem_limit_bytes=32 * 2**20),
        name="keys_backward",
    )(dk_all, dv_all, come, lin, cosine, sine, gain)


def rows_first(left, right):
    return lax.dot_general(
        left, right, (((0,), (0,)), ((), ())), preferred_element_type=jnp.float32
    )


def rows_last(left, right):
    return lax.dot_general(
        left, right, (((1,), (1,)), ((), ())), preferred_element_type=jnp.float32
    )


BOTH = ("dp", "ctx")


def per_device(
    tokens,
    segment_ids,
    w_query,
    key_matrix,
    value_matrix,
    w_out,
    w_gate,
    w_up,
    w_down,
    gain_attn,
    gain_mlp,
    gain_query,
    gain_key,
    out_cot,
):
    width = tokens.shape[1]
    q_width, kv_width, ff = w_query.shape[1], key_matrix.shape[1], w_gate.shape[1]
    q_heads, kv_heads = q_width // D, kv_width // D
    ctx_index = lax.axis_index("ctx")
    tokens_all = lax.all_gather(tokens, "tensor", axis=0, tiled=True)
    gains = jnp.concatenate([gain_attn, gain_mlp, gain_query, gain_key])
    per_gain = (gain_attn.shape[0], gain_mlp.shape[0], gain_query.shape[0], gain_key.shape[0])
    gains_all = lax.all_gather(gains[None, :], BOTH, axis=0, tiled=True).astype(jnp.float32)
    cuts = [0]
    for n in per_gain:
        cuts.append(cuts[-1] + n)
    attn_gain, mlp_gain, query_gain, key_gain = (
        gains_all[:, cuts[j] : cuts[j + 1]].reshape(1, -1) for j in range(4)
    )
    w_qkv = lax.all_gather(
        jnp.concatenate([w_query, key_matrix, value_matrix], axis=1), BOTH, axis=0, tiled=True
    )
    w_rest = lax.all_gather(
        jnp.concatenate([w_out.T, w_gate, w_up, w_down.T], axis=1), BOTH, axis=0, tiled=True
    )
    out_turned = w_rest[:, :q_width]
    gate_up = w_rest[:, q_width : q_width + 2 * ff]
    down_turned = w_rest[:, q_width + 2 * ff :]

    span = tokens_all.shape[0]
    cosine, sine, starts = rotary_own(segment_ids, ctx_index, span)
    lo = starts[::BQ] // BK
    late = starts[BQ - 1 :: BQ]
    start_cols = jnp.broadcast_to(starts[:, None], (span, D))
    start_rows = jnp.broadcast_to(starts[None, :], (8, span))

    norm_one_all, lin, query_rows, kv_rows = qkv_call(
        tokens_all, attn_gain, w_qkv, cosine, sine, query_gain, key_gain, q_heads, kv_heads
    )
    kv_all = jnp.concatenate([from_behind(kv_rows, "ctx", 1), kv_rows], axis=0)
    mixed, inverse = forward_call(lo, late, query_rows, kv_all, start_cols, kv_heads)

    attn_total = lax.psum_scatter(
        rows_last(mixed, out_turned).astype(jnp.bfloat16), "tensor", scatter_dimension=0, tiled=True
    ).astype(jnp.float32)
    rows_in = tokens.astype(jnp.float32)
    middle = rows_in + attn_total
    norm_two = norm_rows(middle, mlp_gain).astype(jnp.bfloat16)
    norm_two_all = lax.all_gather(norm_two, "tensor", axis=0, tiled=True)
    cot_all = lax.all_gather(out_cot, "tensor", axis=0, tiled=True)
    gate_act = jnp.dot(norm_two_all, gate_up[:, :ff], preferred_element_type=jnp.float32)
    up_proj = jnp.dot(norm_two_all, gate_up[:, ff:], preferred_element_type=jnp.float32)
    sigma_gate = jax.nn.sigmoid(gate_act)
    hidden = (gate_act * sigma_gate * up_proj).astype(jnp.bfloat16)
    d_hidden = jnp.dot(cot_all, down_turned, preferred_element_type=jnp.float32)
    d_gate = (d_hidden * up_proj * sigma_gate * (1.0 + gate_act * (1.0 - sigma_gate))).astype(
        jnp.bfloat16
    )
    d_up = (d_hidden * gate_act * sigma_gate).astype(jnp.bfloat16)
    d_both = jnp.concatenate([d_gate, d_up], axis=1)
    d_norm_two = lax.psum_scatter(
        rows_last(d_both, gate_up).astype(jnp.bfloat16), "tensor", scatter_dimension=0, tiled=True
    ).astype(jnp.float32)
    mlp_total = lax.psum_scatter(
        rows_last(hidden, down_turned).astype(jnp.bfloat16),
        "tensor",
        scatter_dimension=0,
        tiled=True,
    ).astype(jnp.float32)
    layer_out = (middle + mlp_total).astype(jnp.bfloat16)
    mlp_grads = lax.psum_scatter(
        jnp.concatenate(
            [
                rows_first(norm_two_all, d_both).astype(jnp.bfloat16),
                rows_first(cot_all, hidden).astype(jnp.bfloat16),
            ],
            axis=1,
        ),
        BOTH,
        scatter_dimension=0,
        tiled=True,
    ).astype(jnp.float32)

    d_middle_norm, mlp_terms = norm_back(middle, mlp_gain, d_norm_two)
    d_middle = out_cot.astype(jnp.float32) + d_middle_norm
    d_middle_all = lax.all_gather(d_middle.astype(jnp.bfloat16), "tensor", axis=0, tiled=True)
    d_mixed = jnp.dot(d_middle_all, out_turned, preferred_element_type=jnp.float32).astype(
        jnp.bfloat16
    )
    grad_out = lax.psum_scatter(
        rows_first(d_middle_all, mixed).astype(jnp.bfloat16), BOTH, scatter_dimension=0, tiled=True
    ).astype(jnp.float32)
    dq_low, dk_all, dv_all, query_terms = backward_call(
        lo, late, query_rows, d_mixed, mixed, inverse, lin, cosine, sine, start_rows,
        query_gain, kv_all, kv_heads,
    )
    come = from_behind(
        jnp.concatenate([dk_all[:span], dv_all[:span]], axis=1).astype(jnp.bfloat16), "ctx", -1
    )
    dkv_low, key_terms = keys_back_call(
        dk_all, dv_all, come, lin, cosine, sine, key_gain, kv_heads
    )
    d_qkv = jnp.concatenate([dq_low, dkv_low], axis=1)
    d_norm_one = lax.psum_scatter(
        rows_last(d_qkv, w_qkv).astype(jnp.bfloat16), "tensor", scatter_dimension=0, tiled=True
    ).astype(jnp.float32)
    qkv_grads = lax.psum_scatter(
        rows_first(norm_one_all, d_qkv).astype(jnp.bfloat16), BOTH, scatter_dimension=0, tiled=True
    ).astype(jnp.float32)
    d_rows_norm, attn_terms = norm_back(rows_in, attn_gain, d_norm_one)
    d_tokens = (d_middle + d_rows_norm).astype(jnp.bfloat16)
    blocks = gains_all.shape[0]
    terms = jnp.concatenate(
        [
            jnp.sum(attn_terms, axis=0).reshape(blocks, -1),
            jnp.sum(mlp_terms, axis=0).reshape(blocks, -1),
            query_terms[0].reshape(blocks, -1),
            key_terms[0].reshape(blocks, -1),
        ],
        axis=1,
    )
    terms = lax.psum(terms, ("dp", "ctx", "tensor"))
    place = lax.axis_index("dp") * lax.axis_size("ctx") + ctx_index
    terms = lax.dynamic_slice_in_dim(terms, place, 1, 0)[0]
    return (
        layer_out,
        d_tokens,
        qkv_grads[:, :q_width],
        qkv_grads[:, q_width : q_width + kv_width],
        qkv_grads[:, q_width + kv_width :],
        grad_out.T,
        mlp_grads[:, :ff],
        mlp_grads[:, ff : 2 * ff],
        mlp_grads[:, 2 * ff :].T,
        terms[cuts[0] : cuts[1]],
        terms[cuts[1] : cuts[2]],
        terms[cuts[2] : cuts[3]],
        terms[cuts[3] : cuts[4]],
    )


def solution(mesh):
    in_specs = (
        P(("dp", "ctx", "tensor"), None),
        P("dp"),
        P(("dp", "ctx"), "tensor"),
        P(("dp", "ctx"), "tensor"),
        P(("dp", "ctx"), "tensor"),
        P("tensor", ("dp", "ctx")),
        P(("dp", "ctx"), "tensor"),
        P(("dp", "ctx"), "tensor"),
        P("tensor", ("dp", "ctx")),
        P(("dp", "ctx")),
        P(("dp", "ctx")),
        P(("dp", "ctx")),
        P(("dp", "ctx")),
        P(("dp", "ctx", "tensor"), None),
    )
    out_specs = (
        P(("dp", "ctx", "tensor"), None),
        P(("dp", "ctx", "tensor"), None),
        P(("dp", "ctx"), "tensor"),
        P(("dp", "ctx"), "tensor"),
        P(("dp", "ctx"), "tensor"),
        P("tensor", ("dp", "ctx")),
        P(("dp", "ctx"), "tensor"),
        P(("dp", "ctx"), "tensor"),
        P("tensor", ("dp", "ctx")),
        P(("dp", "ctx")),
        P(("dp", "ctx")),
        P(("dp", "ctx")),
        P(("dp", "ctx")),
    )
    return jax.shard_map(
        per_device, mesh=mesh, in_specs=in_specs, out_specs=out_specs, check_vma=False
    )
```

time: 1510 us -> 856 us (0.57); the launches traced: 1500 us -> 864 us
  blocking collectives: 270 us -> 63.3 us
  waiting for transfers between devices: 704 us -> 510 us
  matrix products: 239 us -> 93 us
  Pallas kernels: 0 us -> 99.5 us
  other arithmetic: 122 us -> 30.3 us
  local copies, waits for them, and re-layouts: 110 us -> 45 us
  loops' own time: 29.4 us -> 0 us
    all_gather x4 -> x0, blocking collectives: 221 us -> none  [the longest x1 132 us: per_device(): lax.all_gather(gain_mlp, ('dp', 'ctx'), axis=0, tiled=True)]
    dot_general x35 -> x4, matrix products: 168 us -> 34.7 us  [the longest x1 10.8 us: per_device(): jnp.dot(norm_two_all, gate_up[:, ff:], preferred_element_type=jnp.float32)]
    reduce_scatter x9 -> x7, waiting for transfers between devices: 311 us -> 209 us  [the longest x1 77.8 us: per_device(): lax.psum_scatter(rows_last(mixed, out_turned).astype(jnp.bfloat16), 'tens...]
    pallas_call x0 -> x4, Pallas kernels: none -> 99.5 us  [the longest x1 55 us: backward_call(): pl.pallas_call(functools.partial(backward_kernel, span, share), grid_spec...]
    all_gather x6 -> x3, waiting for transfers between devices: 115 us -> 52.5 us  [the longest x1 34.5 us: per_device(): tokens_all = lax.all_gather(tokens, 'tensor', axis=0, tiled=True)]
    psum x1, blocking collectives: 10.2 us -> 39.7 us  [per_device(): terms = lax.psum(terms, ('dp', 'ctx', 'tensor'))]
    reduce_sum x10 -> x2, other arithmetic: 32.4 us -> 5.41 us  [the longest x1 3.32 us: per_device(): jnp.sum(mlp_terms, axis=0).reshape(blocks, -1)]
    convert_element_type x21 -> x2, other arithmetic: 24.8 us -> 1.24 us  [the longest x1 1.23 us: per_device(): mlp_grads = lax.psum_scatter(jnp.concatenate([rows_first(norm_two_all, d_...]
  transfers between devices with their start and end apart: 24 -> 15, of which waited for: 15 -> 12; matrix products, arithmetic and copies ran while one was open for 27% -> 12% of each run, Pallas kernels for 0% -> 12%
where the time goes in v1:
time: 856 us; the launch traced here: 864 us
  waiting for transfers between devices  510 us (60%)
  Pallas kernels  99.5 us (12%)
  matrix products  93 us (11%)
  blocking collectives  63.3 us (7%)
  local copies, waits for them, and re-layouts  45 us (5%)
  other arithmetic  30.3 us (4%)
  between operations  15.5 us (2%)
    ppermute x2, waiting for transfers between devices, from_behind(): return lax.ppermute(shard, axis, pairs)  171 us
    reduce_scatter x1, waiting for transfers between devices, per_device(): lax.psum_scatter(rows_last(mixed, out_turned).astype(jnp.bfloat16), 'tens...  77.8 us
    pallas_call x1, Pallas kernels, backward_call(): pl.pallas_call(functools.partial(backward_kernel, span, share), grid_spec...  55 us
    reduce_scatter x1, waiting for transfers between devices, per_device(): lax.psum_scatter(rows_last(d_both, gate_up).astype(jnp.bfloat16), 'tensor...  44.5 us
    reduce_scatter x1, waiting for transfers between devices, per_device(): lax.psum_scatter(rows_last(d_qkv, w_qkv).astype(jnp.bfloat16), 'tensor',...  42.8 us
    psum x1, blocking collectives, per_device(): terms = lax.psum(terms, ('dp', 'ctx', 'tensor'))  39.7 us
    reduce_scatter x1, waiting for transfers between devices, per_device(): lax.psum_scatter(rows_first(norm_one_all, d_qkv).astype(jnp.bfloat16), BO...  38.8 us
    all_gather x1, waiting for transfers between devices, per_device(): tokens_all = lax.all_gather(tokens, 'tensor', axis=0, tiled=True)  34.5 us
  transfers between devices with their start and end apart: 15, of which 12 were waited for; matrix products, arithmetic and copies ran while one was open for 12% of the time, Pallas kernels for 12%

profile of v1, /device:TPU:0, one launch (start us, length us, event | category | flops | bytes accessed | tf_op | source)
XLA Modules:
  0.0 864.3 jit_solution(15249057403529250028)
XLA Ops:
  15.6 23.6 %all-reduce = bf16[2304]{0:T(1024)(128)(2,1)S(1)} all-reduce(bf16[2304]{0:T(1024)(128)(2,1)S(1)} %dynamic-update-slice), channel_id=2, replica_groups=mesh['dp'=4,'ctx'=2,'tensor'=4] {'dp','ctx'}, use_global_device_ids=true, to_apply=%add | all-reduce | flops 2304 | bytes 9216
  40.9 3.7 fusion.36
  45.2 17.9 %all-gather.10.cloned.1.call-done.w_ref = bf16[1024,1024]{1,0:T(8,128)(2,1)} async-done(((bf16[128,1024]{1,0:T(8,128)(2,1)}), bf16[1024,1024]{1,0:T(8,128)(2,1)}) %all-gather.10.cloned.1.call-update) | async-done | bytes 2097168 | tf_op jit(solution)/shard_map/all_gather | solution.py:401
  63.1 34.5 %all-gather.8.cloned.1.call-done.x_ref = bf16[2048,1024]{1,0:T(8,128)(2,1)} async-done(((bf16[512,1024]{1,0:T(8,128)(2,1)}), bf16[2048,1024]{1,0:T(8,128)(2,1)}) %all-gather.8.cloned.1.call-update) | async-done | bytes 4194320 | tf_op jit(solution)/shard_map/all_gather | solution.py:391
  99.3 11.3 %qkv_forward.1 = (bf16[2048,1024]{1,0:T(8,128)(2,1)S(1)}, f32[2048,768]{1,0:T(8,128)}, bf16[2048,512]{1,0:T(8,128)(2,1)S(1)}, bf16[2048,512]{1,0:T(8,128)(2,1)}) custom-call(bf16[2048,1024]{1,0:T(8,128)(2,1)} %all-gather.8.cloned.1.call-done.x_ref, f32[1,1024]{1,0:T(1,128)S(1)} %bitcast.58, bf16[1024,1024]{1,0:T(8,128)(2,1)S(1)} %copy-done.5, ...), custom_call_target="tpu_custom_call" | custom-call | flops 4294967296 | bytes 24576000 | tf_op jit(solution)/shard_map/qkv_forward/pallas_call | solution.py:103
  114.0 4.8 collective-permute-start
  118.9 65.8 %collective-permute-done = bf16[2048,512]{1,0:T(8,128)(2,1)} collective-permute-done((bf16[2048,512]{1,0:T(8,128)(2,1)}, bf16[2048,512]{1,0:T(8,128)(2,1)}, u32[]{:S(2)}, u32[]{:S(2)}) %collective-permute-start) | collective-permute-done | bytes 2097184 | tf_op jit(solution)/shard_map/ppermute | solution.py:21
  188.7 27.4 %attention_forward.1 = (bf16[2048,512]{1,0:T(8,128)(2,1)S(1)}, f32[2048,512]{1,0:T(8,128)S(1)}) custom-call(s32[8]{0:T(128)S(1)} %and_select_fusion.lo_ref, s32[8]{0:T(128)S(1)} %slice.109.late_ref, bf16[2048,512]{1,0:T(8,128)(2,1)S(1)} %copy-done.12, bf16[4096,512]{1,0:T(8,128)(2,1)S(1)} %constant_dynamic-update-slice_fusion.k_ref.v_ref, ...), custom_call_target="tpu_custom_call" | custom-call | flops 42949672960 | bytes 20971520 | tf_op jit(solution)/shard_map/attention_forward/pallas_call | solution.py:175
  221.4 6.3 convolution_convert_fusion
  228.8 77.8 %reduce-scatter.8.cloned.1.call-done = bf16[512,1024]{1,0:T(8,128)(2,1)} async-done(((bf16[2048,1024]{1,0:T(8,128)(2,1)}), bf16[512,1024]{1,0:T(8,128)(2,1)}) %reduce-scatter.8.cloned.1.call-update) | async-done | bytes 1048592 | tf_op jit(solution)/shard_map/reduce_scatter | solution.py:424
  310.9 31.7 %all-gather.16.cloned.1.call-done = bf16[2048,1024]{1,0:T(8,128)(2,1)} async-done(((bf16[512,1024]{1,0:T(8,128)(2,1)}), bf16[2048,1024]{1,0:T(8,128)(2,1)}) %all-gather.16.cloned.1.call-update) | async-done | bytes 4194320 | tf_op jit(solution)/shard_map/all_gather | solution.py:431
  342.6 8.7 %fusion.31 = f32[768,2048]{1,0:T(8,128)} fusion(bf16[2048,1024]{1,0:T(8,128)(2,1)} %all-gather.16.cloned.1.call-done, bf16[1024,2816]{0,1:T(8,128)(2,1)} %all-gather.12.cloned.1.call-done), kind=kOutput, calls=%fused_computation.60 | convolution fusion | flops 3221225472 | bytes 12058624 | tf_op jit(solution)/shard_map/dot_general | solution.py:436
  351.3 27.9 %all-gather.14.cloned.1.call-done = bf16[2048,1024]{1,0:T(8,128)(2,1)} async-done(((bf16[512,1024]{1,0:T(8,128)(2,1)}), bf16[2048,1024]{1,0:T(8,128)(2,1)}) %all-gather.14.cloned.1.call-update) | async-done | bytes 4194320 | tf_op jit(solution)/shard_map/all_gather | solution.py:430
  379.2 8.9 %fusion.28 = f32[2048,768]{0,1:T(8,128)} fusion(bf16[2048,1024]{1,0:T(8,128)(2,1)} %all-gather.14.cloned.1.call-done, bf16[1024,2816]{0,1:T(8,128)(2,1)} %all-gather.12.cloned.1.call-done), kind=kOutput, calls=%fused_computation.54 | convolution fusion | flops 3221225472 | bytes 12058624 | tf_op jit(solution)/shard_map/dot_general | solution.py:432
  388.1 10.8 %fusion.2 = (bf16[2048,768]{0,1:T(8,128)(2,1)}, bf16[2048,768]{0,1:T(8,128)(2,1)}, bf16[2048,768]{0,1:T(8,128)(2,1)}) fusion(f32[768,2048]{1,0:T(8,128)S(1)} %copy-done.42, f32[2048,768]{0,1:T(8,128)} %fusion.28, bf16[2048,1024]{1,0:T(8,128)(2,1)S(1)} %copy-done.38, bf16[1024,2816]{0,1:T(8,128)(2,1)} %all-gather.12.cloned.1.call-done), kind=kOutput, calls=%fused_computation.5 | convolution fusion | flops 3246391296 | bytes 27787264 | tf_op jit(solution)/shard_map/dot_general | solution.py:433
  399.0 11.3 %fusion.7 = bf16[2048,1024]{1,0:T(8,128)(2,1)} fusion(bf16[2048,768]{0,1:T(8,128)(2,1)} %get-tuple-element.69, bf16[2048,768]{0,1:T(8,128)(2,1)} %get-tuple-element.68, bf16[1024,2816]{0,1:T(8,128)(2,1)S(1)} %bitcast.64), kind=kOutput, calls=%fused_computation.18 | convolution fusion | flops 6457131008 | bytes 13631488 | tf_op jit(solution)/shard_map/dot_general | solution.py:363
  410.6 44.5 %reduce-scatter.12.cloned.1.call-done = bf16[512,1024]{1,0:T(8,128)(2,1)} async-done(((bf16[2048,1024]{1,0:T(8,128)(2,1)}), bf16[512,1024]{1,0:T(8,128)(2,1)}) %reduce-scatter.12.cloned.1.call-update) | async-done | bytes 1048592 | tf_op jit(solution)/shard_map/reduce_scatter | solution.py:442
  460.9 6.8 fusion.30
  467.7 8.4 fusion.8
  478.9 16.5 %all-gather.18.cloned.1.call-done = bf16[2048,1024]{1,0:T(8,128)(2,1)} async-done(((bf16[512,1024]{1,0:T(8,128)(2,1)}), bf16[2048,1024]{1,0:T(8,128)(2,1)}) %all-gather.18.cloned.1.call-update) | async-done | bytes 4194320 | tf_op jit(solution)/shard_map/all_gather | solution.py:467
  495.4 6.2 convolution_convert_fusion.3.do_ref
  501.7 55.0 %attention_backward.1 = (bf16[2048,512]{1,0:T(8,128)(2,1)S(1)}, f32[4096,256]{1,0:T(8,128)}, f32[4096,256]{1,0:T(8,128)}, f32[8,128]{1,0:T(8,128)S(1)}) custom-call(s32[8]{0:T(128)S(1)} %and_select_fusion.lo_ref, s32[8]{0:T(128)S(1)} %slice.109.late_ref, bf16[2048,512]{1,0:T(8,128)(2,1)} %copy-done.11, bf16[2048,512]{1,0:T(8,128)(2,1)} %convolution_convert_fusion.3.do_ref, ...), custom_call_target="tpu_custom_call" | custom-call | flops 107374182400 | bytes 41943040 | tf_op jit(solution)/shard_map/attention_backward/pallas_call | solution.py:280
  569.2 105.6 %collective-permute-done.1.come_ref = bf16[2048,512]{1,0:T(8,128)(2,1)} collective-permute-done((bf16[2048,512]{1,0:T(8,128)(2,1)}, bf16[2048,512]{1,0:T(8,128)(2,1)}, u32[]{:S(2)}, u32[]{:S(2)}) %collective-permute-start.1) | collective-permute-done | bytes 2097184 | tf_op jit(solution)/shard_map/ppermute | solution.py:21
  679.8 5.8 keys_backward.1
  689.4 5.8 convolution_convert_fusion.4
  695.6 8.4 convolution_convert_fusion.2
  704.0 7.9 convolution_convert_fusion.1
  720.7 38.8 %reduce-scatter.16.cloned.1.call-done = bf16[128,1024]{1,0:T(8,128)(2,1)} async-done(((bf16[1024,1024]{1,0:T(8,128)(2,1)}), bf16[128,1024]{1,0:T(8,128)(2,1)}) %reduce-scatter.16.cloned.1.call-update) | async-done | bytes 262160 | tf_op jit(solution)/shard_map/reduce_scatter | solution.py:488
  762.7 42.8 %reduce-scatter.14.cloned.1.call-done = bf16[512,1024]{1,0:T(8,128)(2,1)} async-done(((bf16[2048,1024]{1,0:T(8,128)(2,1)}), bf16[512,1024]{1,0:T(8,128)(2,1)}) %reduce-scatter.14.cloned.1.call-update) | async-done | bytes 1048592 | tf_op jit(solution)/shard_map/reduce_scatter | solution.py:485
  807.7 39.7 %psum.7 = f32[8,288]{1,0:T(8,128)S(1)} all-reduce(f32[8,288]{1,0:T(8,128)S(1)} %pad_maximum_fusion.13), channel_id=1, replica_groups=mesh['dp'=4,'ctx'=2,'tensor'=4] {'dp','ctx','tensor'}, use_global_device_ids=true, to_apply=%region_15.16 | all-reduce | flops 2304 | bytes 18432 | tf_op jit(solution)/shard_map/psum | solution.py:503
  848.6 4.7 reduce-scatter.10.cloned.1.call-done
  853.4 4.0 fusion.15
  (186 shorter events, 75.3 us)
Async XLA Ops:
  7.2 32.3 %copy-start.24 = (s32[4096]{0:T(1024)S(1)}, s32[4096]{0:T(1024)}, u32[]{:S(2)}) copy-start(s32[4096]{0:T(1024)} %param.15) | copy-start | bytes 49156
  7.2 55.9 %all-gather.10.cloned.1.call-start = ((), (), s32[]{:S(2)}) async-start(), calls=%async_computation.8 | async-start | bytes 2359296 | tf_op jit(solution)/shard_map/all_gather | solution.py:401
  9.0 88.7 %all-gather.8.cloned.1.call-start = ((), (), s32[]{:S(2)}) async-start(), calls=%async_computation.7 | async-start | bytes 5242880 | tf_op jit(solution)/shard_map/all_gather | solution.py:391
  9.8 211.6 %all-gather.12.cloned.1.call-start = ((), (), s32[]{:S(2)}) async-start(), calls=%async_computation.9 | async-start | bytes 6488064 | tf_op jit(solution)/shard_map/all_gather | solution.py:404
  13.9 292.6 %reduce-scatter.8.cloned.1.call-start = ((), (), s32[]{:S(2)}) async-start(), calls=%async_computation.10 | async-start | bytes 5242880 | tf_op jit(solution)/shard_map/reduce_scatter | solution.py:424
  40.9 417.5 %copy-start.22 = (f32[1024]{0:T(1024)}, f32[1024]{0:T(1024)S(1)}, u32[]{:S(2)}) copy-start(f32[1024]{0:T(1024)S(1)} %get-tuple-element.84) | copy-start | bytes 12292
  114.0 70.8 %collective-permute-start = (bf16[2048,512]{1,0:T(8,128)(2,1)}, bf16[2048,512]{1,0:T(8,128)(2,1)}, u32[]{:S(2)}, u32[]{:S(2)}) collective-permute-start(bf16[2048,512]{1,0:T(8,128)(2,1)} %get-tuple-element.26), channel_id=1, source_target_pairs={{0,4},{1,5},{2,6},{3,7},{8,12},{9,13},{10,14},{11,15},{16,20},{17,... | collective-permute-start | bytes 6291464 | tf_op jit(solution)/shard_map/ppermute | solution.py:21
  227.7 78.9 %copy-start.14 = (bf16[512,1024]{1,0:T(8,128)(2,1)S(1)}, bf16[512,1024]{1,0:T(8,128)(2,1)}, u32[]{:S(2)}) copy-start(bf16[512,1024]{1,0:T(8,128)(2,1)} %param.14) | copy-start | bytes 3145732
  227.7 114.9 %all-gather.16.cloned.1.call-start = ((), (), s32[]{:S(2)}) async-start(), calls=%async_computation.13 | async-start | bytes 5242880 | tf_op jit(solution)/shard_map/all_gather | solution.py:431
  228.3 150.9 %all-gather.14.cloned.1.call-start = ((), (), s32[]{:S(2)}) async-start(), calls=%async_computation.11 | async-start | bytes 5242880 | tf_op jit(solution)/shard_map/all_gather | solution.py:430
  308.2 150.1 %copy-start.25 = (f32[512]{0:T(512)}, f32[512]{0:T(512)S(1)}, u32[]{:S(2)}) copy-start(f32[512]{0:T(512)S(1)} %get-tuple-element.94) | copy-start | bytes 6148
  308.2 150.1 %copy-start.28 = (f32[512]{0:T(512)}, f32[512]{0:T(512)S(1)}, u32[]{:S(2)}) copy-start(f32[512]{0:T(512)S(1)} %get-tuple-element.93) | copy-start | bytes 6148
  310.8 144.2 %reduce-scatter.12.cloned.1.call-start = ((), (), s32[]{:S(2)}) async-start(), calls=%async_computation.14 | async-start | bytes 5242880 | tf_op jit(solution)/shard_map/reduce_scatter | solution.py:442
  379.2 19.8 %slice-start = ((s8[5767168]{0:T(1024)(128)(4,1)}), s8[4194304]{0:T(1024)(128)(4,1)S(1)}, s32[]{:S(2)}) async-start(s8[5767168]{0:T(1024)(128)(4,1)} %bitcast.63), calls=%async_computation.20 | async-start | bytes 8388608
  388.1 10.9 %slice-start.1 = ((s8[5767168]{0:T(1024)(128)(4,1)}), s8[1572864]{0:T(1024)(128)(4,1)S(1)}, s32[]{:S(2)}) async-start(s8[5767168]{0:T(1024)(128)(4,1)} %bitcast.63), calls=%async_computation.21 | async-start | bytes 3145728
  410.3 85.1 %all-gather.18.cloned.1.call-start = ((), (), s32[]{:S(2)}) async-start(), calls=%async_computation.15 | async-start | bytes 5242880 | tf_op jit(solution)/shard_map/all_gather | solution.py:467
  460.8 251.9 %reduce-scatter.20.cloned.1.call-start = ((), (), s32[]{:S(2)}) async-start(), calls=%async_computation.19 | async-start | bytes 5308416 | tf_op jit(solution)/shard_map/reduce_scatter | solution.py:452
  478.7 240.2 %reduce-scatter.18.cloned.1.call-start = ((), (), s32[]{:S(2)}) async-start(), calls=%async_computation.18 | async-start | bytes 1179648 | tf_op jit(solution)/shard_map/reduce_scatter | solution.py:471
  562.4 112.4 %collective-permute-start.1 = (bf16[2048,512]{1,0:T(8,128)(2,1)}, bf16[2048,512]{1,0:T(8,128)(2,1)}, u32[]{:S(2)}, u32[]{:S(2)}) collective-permute-start(bf16[2048,512]{1,0:T(8,128)(2,1)} %pad_maximum_fusion.8), channel_id=1, source_target_pairs={{4,0},{5,1},{6,2},{7,3},{12,8},{13,9},{14,10},{15,11},{20,16},{21,... | collective-permute-start | bytes 6291464 | tf_op jit(solution)/shard_map/ppermute | solution.py:21
  567.1 192.4 %reduce-scatter.16.cloned.1.call-start = ((), (), s32[]{:S(2)}) async-start(), calls=%async_computation.17 | async-start | bytes 2359296 | tf_op jit(solution)/shard_map/reduce_scatter | solution.py:488
  567.1 107.7 %copy-start = (f32[4096,256]{1,0:T(8,128)S(1)}, f32[4096,256]{1,0:T(8,128)}, u32[]{:S(2)}) copy-start(f32[4096,256]{1,0:T(8,128)} %get-tuple-element.31.dk_ref) | copy-start | bytes 12582916
  695.2 110.3 %reduce-scatter.14.cloned.1.call-start = ((), (), s32[]{:S(2)}) async-start(), calls=%async_computation.16 | async-start | bytes 5242880 | tf_op jit(solution)/shard_map/reduce_scatter | solution.py:485
  704.0 149.3 %reduce-scatter.10.cloned.1.call-start = ((), (), s32[]{:S(2)}) async-start(), calls=%async_computation.12 | async-start | bytes 5242880 | tf_op jit(solution)/shard_map/reduce_scatter | solution.py:445
  712.6 92.9 %copy-start.15 = (bf16[512,1024]{1,0:T(8,128)(2,1)S(1)}, bf16[512,1024]{1,0:T(8,128)(2,1)}, u32[]{:S(2)}) copy-start(bf16[512,1024]{1,0:T(8,128)(2,1)} %param.14) | copy-start | bytes 3145732
  712.6 92.9 %copy-start.27 = (f32[1024]{0:T(1024)S(1)}, f32[1024]{0:T(1024)}, u32[]{:S(2)}) copy-start(f32[1024]{0:T(1024)} %get-tuple-element.83) | copy-start | bytes 12292
  714.7 93.0 %copy-start.32 = (f32[1024]{0:T(1024)S(1)}, f32[1024]{0:T(1024)}, u32[]{:S(2)}) copy-start(f32[1024]{0:T(1024)} %get-tuple-element.63) | copy-start | bytes 12292
  714.7 138.7 %copy-start.17 = (bf16[512,1024]{1,0:T(8,128)(2,1)S(1)}, bf16[512,1024]{1,0:T(8,128)(2,1)}, u32[]{:S(2)}) copy-start(bf16[512,1024]{1,0:T(8,128)(2,1)} %reduce-scatter.8.cloned.1.call-done) | copy-start | bytes 3145732
  714.7 138.7 %copy-start.19 = (bf16[512,1024]{1,0:T(8,128)(2,1)S(1)}, bf16[512,1024]{1,0:T(8,128)(2,1)}, u32[]{:S(2)}) copy-start(bf16[512,1024]{1,0:T(8,128)(2,1)} %param.27) | copy-start | bytes 3145732
  714.7 138.7 %copy-start.23 = (f32[1024]{0:T(1024)S(1)}, f32[1024]{0:T(1024)}, u32[]{:S(2)}) copy-start(f32[1024]{0:T(1024)} %copy-done.22) | copy-start | bytes 12292
  714.7 138.7 %copy-start.26 = (f32[512]{0:T(512)S(1)}, f32[512]{0:T(512)}, u32[]{:S(2)}) copy-start(f32[512]{0:T(512)} %copy-done.25) | copy-start | bytes 6148
  714.7 138.7 %copy-start.29 = (f32[512]{0:T(512)S(1)}, f32[512]{0:T(512)}, u32[]{:S(2)}) copy-start(f32[512]{0:T(512)} %copy-done.28) | copy-start | bytes 6148
  714.7 138.7 %copy-start.31 = (f32[512]{0:T(512)S(1)}, f32[512]{0:T(512)}, u32[]{:S(2)}) copy-start(f32[512]{0:T(512)} %copy-done.30) | copy-start | bytes 6148
  (30 other events, 135.0 us)
Sparse Core Ops, SparseCore 0:
  10.8 52.3 all-gather.9
  64.7 32.9 all-gather.7
  100.3 93.5 all-gather.11
  227.8 78.7 reduce-scatter.7
  308.1 34.4 all-gather.15
  344.6 34.4 all-gather.13
  410.5 44.5 reduce-scatter.11
  460.9 34.4 all-gather.17
  499.1 95.3 reduce-scatter.19
  598.3 89.0 reduce-scatter.17
  695.4 64.0 reduce-scatter.15
  762.0 43.4 reduce-scatter.13
  808.1 45.2 reduce-scatter.9

commit v2 on v1

--- a/solution.py
+++ b/solution.py
@@ -365,6 +365,48 @@
     )
 
 
+def tensor_gather(block):
+    if lax.axis_size("tensor") != 4:
+        return lax.all_gather(block, "tensor", axis=0, tiled=True)
+    index = lax.axis_index("tensor")
+    core, chip = index % 2, index // 2
+    over = lax.ppermute(block, "tensor", [(t, t ^ 2) for t in range(4)])
+    near = lax.ppermute(block, "tensor", [(t, t ^ 1) for t in range(4)])
+    far = lax.ppermute(over, "tensor", [(t, t ^ 1) for t in range(4)])
+
+    def order(which, one, two):
+        return jnp.where(which == 0, jnp.concatenate([one, two]), jnp.concatenate([two, one]))
+
+    return order(chip, order(core, block, near), order(core, over, far))
+
+
+def tensor_scatter(total):
+    if lax.axis_size("tensor") != 4:
+        return lax.psum_scatter(
+            total.astype(jnp.bfloat16), "tensor", scatter_dimension=0, tiled=True
+        ).astype(jnp.float32)
+    index = lax.axis_index("tensor")
+    core, chip = index % 2, index // 2
+    rows, width = total.shape
+    blocks = total.astype(jnp.bfloat16).reshape(2, 2, rows // 4, width)
+
+    def pick(i, j):
+        return lax.dynamic_slice(blocks, (i, j, 0, 0), (1, 1, rows // 4, width))[0, 0]
+
+    near = [(t, t ^ 1) for t in range(4)]
+    far_came = lax.ppermute(pick(1 - chip, 1 - core), "tensor", near)
+    own_came = lax.ppermute(pick(chip, 1 - core), "tensor", near)
+    far_sum = pick(1 - chip, core).astype(jnp.float32) + far_came.astype(jnp.float32)
+    over = lax.ppermute(
+        far_sum.astype(jnp.bfloat16), "tensor", [(t, t ^ 2) for t in range(4)]
+    )
+    return (
+        pick(chip, core).astype(jnp.float32)
+        + own_came.astype(jnp.float32)
+        + over.astype(jnp.float32)
+    )
+
+
 BOTH = ("dp", "ctx")
 
 
@@ -388,7 +430,7 @@
     q_width, kv_width, ff = w_query.shape[1], key_matrix.shape[1], w_gate.shape[1]
     q_heads, kv_heads = q_width // D, kv_width // D
     ctx_index = lax.axis_index("ctx")
-    tokens_all = lax.all_gather(tokens, "tensor", axis=0, tiled=True)
+    tokens_all = tensor_gather(tokens)
     gains = jnp.concatenate([gain_attn, gain_mlp, gain_query, gain_key])
     per_gain = (gain_attn.shape[0], gain_mlp.shape[0], gain_query.shape[0], gain_key.shape[0])
     gains_all = lax.all_gather(gains[None, :], BOTH, axis=0, tiled=True).astype(jnp.float32)
@@ -421,13 +463,11 @@
     kv_all = jnp.concatenate([from_behind(kv_rows, "ctx", 1), kv_rows], axis=0)
     mixed, inverse = forward_call(lo, late, query_rows, kv_all, start_cols, kv_heads)
 
-    attn_total = lax.psum_scatter(
-        rows_last(mixed, out_turned).astype(jnp.bfloat16), "tensor", scatter_dimension=0, tiled=True
-    ).astype(jnp.float32)
+    attn_total = tensor_scatter(rows_last(mixed, out_turned))
     rows_in = tokens.astype(jnp.float32)
     middle = rows_in + attn_total
     norm_two = norm_rows(middle, mlp_gain).astype(jnp.bfloat16)
-    norm_two_all = lax.all_gather(norm_two, "tensor", axis=0, tiled=True)
+    norm_two_all = tensor_gather(norm_two)
     cot_all = lax.all_gather(out_cot, "tensor", axis=0, tiled=True)
     gate_act = jnp.dot(norm_two_all, gate_up[:, :ff], preferred_element_type=jnp.float32)
     up_proj = jnp.dot(norm_two_all, gate_up[:, ff:], preferred_element_type=jnp.float32)
@@ -439,16 +479,8 @@
     )
     d_up = (d_hidden * gate_act * sigma_gate).astype(jnp.bfloat16)
     d_both = jnp.concatenate([d_gate, d_up], axis=1)
-    d_norm_two = lax.psum_scatter(
-        rows_last(d_both, gate_up).astype(jnp.bfloat16), "tensor", scatter_dimension=0, tiled=True
-    ).astype(jnp.float32)
-    mlp_total = lax.psum_scatter(
-        rows_last(hidden, down_turned).astype(jnp.bfloat16),
-        "tensor",
-        scatter_dimension=0,
-        tiled=True,
-    ).astype(jnp.float32)
-    layer_out = (middle + mlp_total).astype(jnp.bfloat16)
+    d_norm_two = tensor_scatter(rows_last(d_both, gate_up))
+    mlp_part = rows_last(hidden, down_turned).astype(jnp.bfloat16)
     mlp_grads = lax.psum_scatter(
         jnp.concatenate(
             [
@@ -464,10 +496,12 @@
 
     d_middle_norm, mlp_terms = norm_back(middle, mlp_gain, d_norm_two)
     d_middle = out_cot.astype(jnp.float32) + d_middle_norm
-    d_middle_all = lax.all_gather(d_middle.astype(jnp.bfloat16), "tensor", axis=0, tiled=True)
+    d_middle_all = tensor_gather(d_middle.astype(jnp.bfloat16))
     d_mixed = jnp.dot(d_middle_all, out_turned, preferred_element_type=jnp.float32).astype(
         jnp.bfloat16
     )
+    mlp_part, d_mixed = lax.optimization_barrier((mlp_part, d_mixed))
+    layer_out = (middle + tensor_scatter(mlp_part)).astype(jnp.bfloat16)
     grad_out = lax.psum_scatter(
         rows_first(d_middle_all, mixed).astype(jnp.bfloat16), BOTH, scatter_dimension=0, tiled=True
     ).astype(jnp.float32)
@@ -475,6 +509,7 @@
         lo, late, query_rows, d_mixed, mixed, inverse, lin, cosine, sine, start_rows,
         query_gain, kv_all, kv_heads,
     )
+    dk_all, dv_all, layer_out = lax.optimization_barrier((dk_all, dv_all, layer_out))
     come = from_behind(
         jnp.concatenate([dk_all[:span], dv_all[:span]], axis=1).astype(jnp.bfloat16), "ctx", -1
     )
@@ -482,9 +517,7 @@
         dk_all, dv_all, come, lin, cosine, sine, key_gain, kv_heads
     )
     d_qkv = jnp.concatenate([dq_low, dkv_low], axis=1)
-    d_norm_one = lax.psum_scatter(
-        rows_last(d_qkv, w_qkv).astype(jnp.bfloat16), "tensor", scatter_dimension=0, tiled=True
-    ).astype(jnp.float32)
+    d_norm_one = tensor_scatter(rows_last(d_qkv, w_qkv))
     qkv_grads = lax.psum_scatter(
         rows_first(norm_one_all, d_qkv).astype(jnp.bfloat16), BOTH, scatter_dimension=0, tiled=True
     ).astype(jnp.float32)

time: 856 us -> 739 us (0.86)
  waiting for transfers between devices: 510 us -> 332 us
  other arithmetic: 30.3 us -> 68 us
  blocking collectives: 63.3 us -> 88.9 us
  Pallas kernels: 99.5 us -> 82.7 us
    reduce_scatter x4 -> x0, waiting for transfers between devices: 170 us -> none  [the longest x1 77.8 us: per_device(): lax.psum_scatter(rows_last(mixed, out_turned).astype(jnp.bfloat16), 'tens...]
    ppermute x0 -> x21, waiting for transfers between devices: none -> 142 us  [the longest x4 82 us: tensor_scatter(): lax.ppermute(far_sum.astype(jnp.bfloat16), 'tensor', [(t, t ^ 2) for t in...]
    all_gather x3 -> x0, waiting for transfers between devices: 78.9 us -> none  [the longest x1 34.5 us: per_device(): tokens_all = lax.all_gather(tokens, 'tensor', axis=0, tiled=True)]
    reduce_scatter x1, waiting for transfers between devices: 38.8 us -> 0.01 us  [per_device(): lax.psum_scatter(rows_first(norm_one_all, d_qkv).astype(jnp.bfloat16), BO...]
    all_gather x1, waiting for transfers between devices: 31.7 us -> 0.01 us  [per_device(): cot_all = lax.all_gather(out_cot, 'tensor', axis=0, tiled=True)]
    psum x1, blocking collectives: 39.7 us -> 67 us  [per_device(): terms = lax.psum(terms, ('dp', 'ctx', 'tensor'))]
    select_n x0 -> x7, other arithmetic: none -> 22.9 us  [order(): jnp.where(which == 0, jnp.concatenate([one, two]), jnp.concatenate([two,...]
    convert_element_type x1 -> x6, other arithmetic: 1.82 us -> 15.7 us  [the longest x4 7.56 us: tensor_scatter(): far_sum.astype(jnp.bfloat16)]
  transfers between devices with their start and end apart: 15 -> 29, of which waited for: 12 -> 12; matrix products, arithmetic and copies ran while one was open for 12% -> 18% of each run, Pallas kernels for 12% -> 11%
where the time goes in v2:
time: 739 us; the launch traced here: 741 us
  waiting for transfers between devices  332 us (45%)
  matrix products  98.6 us (13%)
  blocking collectives  88.9 us (12%)
  Pallas kernels  82.7 us (11%)
  other arithmetic  68 us (9%)
  local copies, waits for them, and re-layouts  41.4 us (6%)
  between operations  15.7 us (2%)
  starting transfers between devices  13.9 us (2%)
    ppermute x2, waiting for transfers between devices, from_behind(): return lax.ppermute(shard, axis, pairs)  184 us
    ppermute x4, waiting for transfers between devices, tensor_scatter(): lax.ppermute(far_sum.astype(jnp.bfloat16), 'tensor', [(t, t ^ 2) for t in...  82 us
    psum x1, blocking collectives, per_device(): terms = lax.psum(terms, ('dp', 'ctx', 'tensor'))  67 us
    ppermute x3, waiting for transfers between devices, tensor_gather(): over = lax.ppermute(block, 'tensor', [(t, t ^ 2) for t in range(4)])  49.1 us
    pallas_call x1, Pallas kernels, backward_call(): pl.pallas_call(functools.partial(backward_kernel, span, share), grid_spec...  46.3 us
    dot_general x4, matrix products, rows_last(): lax.dot_general(left, right, (((1,), (1,)), ((), ())), preferred_element_...  33.5 us
    dot_general x4, matrix products, rows_first(): lax.dot_general(left, right, (((0,), (0,)), ((), ())), preferred_element_...  24.4 us
    select_n x7, other arithmetic, order(): jnp.where(which == 0, jnp.concatenate([one, two]), jnp.concatenate([two,...  22.9 us
  transfers between devices with their start and end apart: 29, of which 12 were waited for; matrix products, arithmetic and copies ran while one was open for 18% of the time, Pallas kernels for 11%

profile of v2, /device:TPU:0, one launch (start us, length us, event | category | flops | bytes accessed | tf_op | source)
XLA Modules:
  0.0 741.5 jit_solution(14633644597537170067)
XLA Ops:
  18.5 22.0 %all-reduce = bf16[2304]{0:T(1024)(128)(2,1)S(1)} all-reduce(bf16[2304]{0:T(1024)(128)(2,1)S(1)} %dynamic-update-slice), channel_id=2, replica_groups=mesh['dp'=4,'ctx'=2,'tensor'=4] {'dp','ctx'}, use_global_device_ids=true, to_apply=%add | all-reduce | flops 2304 | bytes 9216
  41.7 3.7 fusion.38
  52.7 3.8 maximum_select_fusion.x_ref
  56.5 6.6 all-gather.5.cloned.1.call-done.w_ref
  64.7 11.2 %qkv_forward.1 = (bf16[2048,1024]{1,0:T(8,128)(2,1)S(1)}, f32[2048,768]{1,0:T(8,128)}, bf16[2048,512]{1,0:T(8,128)(2,1)S(1)}, bf16[2048,512]{1,0:T(8,128)(2,1)}) custom-call(bf16[2048,1024]{1,0:T(8,128)(2,1)} %maximum_select_fusion.x_ref, f32[1,1024]{1,0:T(1,128)S(1)} %bitcast.113, bf16[1024,1024]{1,0:T(8,128)(2,1)S(1)} %copy-done.14, ...), custom_call_target="tpu_custom_call" | custom-call | flops 4294967296 | bytes 24576000 | tf_op jit(solution)/shard_map/qkv_forward/pallas_call | solution.py:103
  82.3 65.6 %collective-permute-done.3 = bf16[2048,512]{1,0:T(8,128)(2,1)S(1)} collective-permute-done((bf16[2048,512]{1,0:T(8,128)(2,1)}, bf16[2048,512]{1,0:T(8,128)(2,1)S(1)}, u32[]{:S(2)}, u32[]{:S(2)}) %collective-permute-start.3) | collective-permute-done | bytes 2097184 | tf_op jit(solution)/shard_map/ppermute | solution.py:21
  150.3 21.8 %attention_forward.1 = (bf16[2048,512]{1,0:T(8,128)(2,1)S(1)}, f32[2048,512]{1,0:T(8,128)S(1)}) custom-call(s32[8]{0:T(128)S(1)} %and_select_fusion.lo_ref, s32[8]{0:T(128)S(1)} %slice.109.late_ref, bf16[2048,512]{1,0:T(8,128)(2,1)S(1)} %copy-done.20, bf16[4096,512]{1,0:T(8,128)(2,1)S(1)} %constant_dynamic-update-slice_fusion.k_ref.v_ref, ...), custom_call_target="tpu_custom_call" | custom-call | flops 42949672960 | bytes 20971520 | tf_op jit(solution)/shard_map/attention_forward/pallas_call | solution.py:175
  176.2 6.4 convolution_convert_fusion
  186.4 4.0 collective-permute-done.5
  193.7 39.7 %collective-permute-done.6 = bf16[512,1024]{1,0:T(8,128)(2,1)S(1)} collective-permute-done((bf16[512,1024]{1,0:T(8,128)(2,1)S(1)}, bf16[512,1024]{1,0:T(8,128)(2,1)S(1)}, u32[]{:S(2)}, u32[]{:S(2)}) %collective-permute-start.6) | collective-permute-done | bytes 1048608 | tf_op jit(solution)/shard_map/ppermute | solution.py:400
  233.4 3.7 multiply_reduce_fusion.2
  239.3 24.7 %collective-permute-done.8 = bf16[512,1024]{1,0:T(8,128)(2,1)} collective-permute-done((bf16[512,1024]{1,0:T(8,128)(2,1)S(1)}, bf16[512,1024]{1,0:T(8,128)(2,1)}, u32[]{:S(2)}, u32[]{:S(2)}) %collective-permute-start.8) | collective-permute-done | bytes 1048608 | tf_op jit(solution)/shard_map/ppermute | solution.py:373
  264.0 8.8 %fusion.33 = f32[768,2048]{1,0:T(8,128)} fusion(bf16[2048,1024]{1,0:T(8,128)(2,1)} %all-gather.9.cloned.1.call-done, bf16[1024,2816]{0,1:T(8,128)(2,1)} %all-gather.7.cloned.1.call-done), kind=kOutput, calls=%fused_computation.78 | convolution fusion | flops 3221225472 | bytes 12058624 | tf_op jit(solution)/shard_map/dot_general | solution.py:476
  278.9 10.2 %fusion.30 = f32[2048,768]{0,1:T(8,128)} fusion(bf16[1024,2816]{0,1:T(8,128)(2,1)} %all-gather.7.cloned.1.call-done, bf16[1024,1024]{1,0:T(8,128)(2,1)S(1)} %maximum_select_fusion.6, bf16[1024,1024]{1,0:T(8,128)(2,1)S(1)} %maximum_select_fusion.5, pred[]{:T(512)S(6)} %eq.21), kind=kOutput, calls=%fused_computation.72 | convolution fusion | flops 3240099840 | bytes 12058625 | tf_op jit(solution)/shard_map/dot_general | solution.py:472
  289.0 14.1 %fusion.2 = (bf16[2048,768]{0,1:T(8,128)(2,1)}, bf16[2048,768]{0,1:T(8,128)(2,1)}, bf16[2048,768]{0,1:T(8,128)(2,1)}) fusion(f32[768,2048]{1,0:T(8,128)} %fusion.33, f32[2048,768]{0,1:T(8,128)} %fusion.30, bf16[1024,2816]{0,1:T(8,128)(2,1)} %all-gather.7.cloned.1.call-done, bf16[1024,1024]{1,0:T(8,128)(2,1)S(1)} %maximum_select_fusion.6, ...), kind=kOutput, calls=%fused_computation.5 | convolution fusion | flops 3265265664 | bytes 27787264 | tf_op jit(solution)/shard_map/dot_general | solution.py:473
  303.2 10.5 %fusion.7 = bf16[2048,1024]{1,0:T(8,128)(2,1)S(1)} fusion(bf16[2048,768]{0,1:T(8,128)(2,1)} %get-tuple-element.82, bf16[2048,768]{0,1:T(8,128)(2,1)} %get-tuple-element.81, bf16[1024,2816]{0,1:T(8,128)(2,1)} %all-gather.7.cloned.1.call-done), kind=kOutput, calls=%fused_computation.21 | convolution fusion | flops 6457131008 | bytes 13631488 | tf_op jit(solution)/shard_map/dot_general | solution.py:363
  318.2 24.4 %collective-permute-done.12 = bf16[512,1024]{1,0:T(8,128)(2,1)S(1)} collective-permute-done((bf16[512,1024]{1,0:T(8,128)(2,1)S(1)}, bf16[512,1024]{1,0:T(8,128)(2,1)S(1)}, u32[]{:S(2)}, u32[]{:S(2)}) %collective-permute-start.12) | collective-permute-done | bytes 1048608 | tf_op jit(solution)/shard_map/ppermute | solution.py:400
  345.8 3.8 fusion.44
  349.9 24.4 %collective-permute-done.14 = bf16[512,1024]{1,0:T(8,128)(2,1)} collective-permute-done((bf16[512,1024]{1,0:T(8,128)(2,1)S(1)}, bf16[512,1024]{1,0:T(8,128)(2,1)}, u32[]{:S(2)}, u32[]{:S(2)}) %collective-permute-start.14) | collective-permute-done | bytes 1048608 | tf_op jit(solution)/shard_map/ppermute | solution.py:373
  374.3 11.4 %fusion.8 = bf16[1024,1536]{1,0:T(8,128)(2,1)} fusion(bf16[2048,768]{0,1:T(8,128)(2,1)} %get-tuple-element.82, bf16[2048,768]{0,1:T(8,128)(2,1)} %get-tuple-element.81, bf16[1024,1024]{1,0:T(8,128)(2,1)S(1)} %maximum_select_fusion.6, bf16[1024,1024]{1,0:T(8,128)(2,1)S(1)} %maximum_select_fusion.5, pred[]{:T(512)S(6)} %eq.21), kind=kOutput, calls=%fused_computation.22 | convolution fusion | flops 6475481088 | bytes 13631489 | tf_op jit(solution)/shard_map/dot_general | solution.py:357
  385.7 8.2 %convolution_convert_fusion.1 = bf16[2048,1024]{1,0:T(8,128)(2,1)} fusion(bf16[2048,768]{0,1:T(8,128)(2,1)} %get-tuple-element.83, bf16[1024,2816]{0,1:T(8,128)(2,1)} %all-gather.7.cloned.1.call-done), kind=kOutput, calls=%fused_computation.24 | convolution fusion | flops 3223322624 | bytes 8912896 | tf_op jit(solution)/shard_map/dot_general | solution.py:363
  396.5 4.0 maximum_select_fusion.8
  405.3 7.6 %convolution_convert_fusion.3.do_ref = bf16[2048,512]{1,0:T(8,128)(2,1)} fusion(bf16[1024,2816]{0,1:T(8,128)(2,1)} %all-gather.7.cloned.1.call-done, bf16[1024,1024]{1,0:T(8,128)(2,1)} %copy-done.30, bf16[1024,1024]{1,0:T(8,128)(2,1)} %copy-done.29, pred[]{:T(512)S(6)} %eq.21), kind=kOutput, calls=%fused_computation.27 | convolution fusion | flops 2167406592 | bytes 7340033 | tf_op jit(solution)/shard_map/dot_general | solution.py:500
  415.8 3.7 fusion.32
  425.8 46.3 %attention_backward.1 = (bf16[2048,512]{1,0:T(8,128)(2,1)S(1)}, f32[4096,256]{1,0:T(8,128)}, f32[4096,256]{1,0:T(8,128)}, f32[8,128]{1,0:T(8,128)S(1)}) custom-call(s32[8]{0:T(128)S(1)} %and_select_fusion.lo_ref, s32[8]{0:T(128)S(1)} %slice.109.late_ref, bf16[2048,512]{1,0:T(8,128)(2,1)} %copy-done.19, bf16[2048,512]{1,0:T(8,128)(2,1)} %convolution_convert_fusion.3.do_ref, ...), custom_call_target="tpu_custom_call" | custom-call | flops 107374182400 | bytes 41943040 | tf_op jit(solution)/shard_map/attention_backward/pallas_call | solution.py:280
  473.3 4.4 fusion.23
  481.6 118.4 %collective-permute-done.19.come_ref = bf16[2048,512]{1,0:T(8,128)(2,1)S(1)} collective-permute-done((bf16[2048,512]{1,0:T(8,128)(2,1)S(1)}, bf16[2048,512]{1,0:T(8,128)(2,1)S(1)}, u32[]{:S(2)}, u32[]{:S(2)}) %collective-permute-start.19) | collective-permute-done | bytes 2097184 | tf_op jit(solution)/shard_map/ppermute | solution.py:21
  607.1 5.9 convolution_convert_fusion.4
  613.0 8.4 %convolution_convert_fusion.2 = bf16[2048,1024]{1,0:T(8,128)(2,1)} fusion(bf16[2048,1024]{1,0:T(8,128)(2,1)} %copy-done.31, bf16[1024,1024]{1,0:T(8,128)(2,1)S(1)} %copy-done.15), kind=kOutput, calls=%fused_computation.25 | convolution fusion | flops 4297064448 | bytes 10485760 | tf_op jit(solution)/shard_map/dot_general | solution.py:363
  638.6 17.8 %collective-permute-done.22 = bf16[512,1024]{1,0:T(8,128)(2,1)} collective-permute-done((bf16[512,1024]{1,0:T(8,128)(2,1)}, bf16[512,1024]{1,0:T(8,128)(2,1)}, u32[]{:S(2)}, u32[]{:S(2)}) %collective-permute-start.22) | collective-permute-done | bytes 1048608 | tf_op jit(solution)/shard_map/ppermute | solution.py:400
  659.4 67.0 %psum.7 = f32[8,288]{1,0:T(8,128)S(1)} all-reduce(f32[8,288]{1,0:T(8,128)S(1)} %pad_maximum_fusion.13), channel_id=1, replica_groups=mesh['dp'=4,'ctx'=2,'tensor'=4] {'dp','ctx','tensor'}, use_global_device_ids=true, to_apply=%region_11.12 | all-reduce | flops 2304 | bytes 18432 | tf_op jit(solution)/shard_map/psum | solution.py:536
  727.5 3.7 fusion.14
  (227 shorter events, 109.6 us)
Async XLA Ops:
  7.3 55.9 %all-gather.5.cloned.1.call-start = ((), (), s32[]{:S(2)}) async-start(), calls=%async_computation.3 | async-start | bytes 2359296 | tf_op jit(solution)/shard_map/all_gather | solution.py:443
  9.1 167.1 %all-gather.7.cloned.1.call-start = ((), (), s32[]{:S(2)}) async-start(), calls=%async_computation.4 | async-start | bytes 6488064 | tf_op jit(solution)/shard_map/all_gather | solution.py:446
  13.3 250.8 %all-gather.9.cloned.1.call-start = ((), (), s32[]{:S(2)}) async-start(), calls=%async_computation.5 | async-start | bytes 5242880 | tf_op jit(solution)/shard_map/all_gather | solution.py:471
  13.3 28.1 %collective-permute-start.1 = (bf16[512,1024]{1,0:T(8,128)(2,1)S(1)}, bf16[512,1024]{1,0:T(8,128)(2,1)}, u32[]{:S(2)}, u32[]{:S(2)}) collective-permute-start(bf16[512,1024]{1,0:T(8,128)(2,1)S(1)} %copy-done.22), channel_id=1, source_target_pairs={{0,2},{1,3},{2,0},{3,1},{4,6},{5,7},{6,4},{7,5},{8,10},{9,11},{10,... | collective-permute-start | bytes 3145736 | tf_op jit(solution)/shard_map/ppermute | solution.py:373
  16.3 29.7 %collective-permute-start = (bf16[512,1024]{1,0:T(8,128)(2,1)S(1)}, bf16[512,1024]{1,0:T(8,128)(2,1)}, u32[]{:S(2)}, u32[]{:S(2)}) collective-permute-start(bf16[512,1024]{1,0:T(8,128)(2,1)S(1)} %copy-done.22), channel_id=1, source_target_pairs={{0,1},{1,0},{2,3},{3,2},{4,5},{5,4},{6,7},{7,6},{8,9},{9,8},{10,11... | collective-permute-start | bytes 3145736 | tf_op jit(solution)/shard_map/ppermute | solution.py:374
  41.4 8.0 %collective-permute-start.2 = (bf16[512,1024]{1,0:T(8,128)(2,1)}, bf16[512,1024]{1,0:T(8,128)(2,1)}, u32[]{:S(2)}, u32[]{:S(2)}) collective-permute-start(bf16[512,1024]{1,0:T(8,128)(2,1)} %collective-permute-done.1), channel_id=1, source_target_pairs={{0,1},{1,0},{2,3},{3,2},{4,5},{5,4},{6,7},{7,6},{8,9},{9,8},{10,11... | collective-permute-start | bytes 3145736 | tf_op jit(solution)/shard_map/ppermute | solution.py:375
  79.3 68.7 %collective-permute-start.3 = (bf16[2048,512]{1,0:T(8,128)(2,1)}, bf16[2048,512]{1,0:T(8,128)(2,1)S(1)}, u32[]{:S(2)}, u32[]{:S(2)}) collective-permute-start(bf16[2048,512]{1,0:T(8,128)(2,1)} %get-tuple-element.31), channel_id=1, source_target_pairs={{0,4},{1,5},{2,6},{3,7},{8,12},{9,13},{10,14},{11,15},{16,20},{17,... | collective-permute-start | bytes 6291464 | tf_op jit(solution)/shard_map/ppermute | solution.py:21
  81.9 550.2 %reduce-scatter.6.cloned.1.call-start = ((), (), s32[]{:S(2)}) async-start(), calls=%async_computation.7 | async-start | bytes 1179648 | tf_op jit(solution)/shard_map/reduce_scatter | solution.py:505
  176.2 224.3 %copy-start.18 = (bf16[2048,512]{1,0:T(8,128)(2,1)}, bf16[2048,512]{1,0:T(8,128)(2,1)S(1)}, u32[]{:S(2)}) copy-start(bf16[2048,512]{1,0:T(8,128)(2,1)S(1)} %get-tuple-element.32.o_ref) | copy-start | bytes 6291460
  185.9 4.5 collective-permute-start.5
  185.9 7.8 %collective-permute-start.4 = (bf16[512,1024]{1,0:T(8,128)(2,1)}, bf16[512,1024]{1,0:T(8,128)(2,1)S(1)}, u32[]{:S(2)}, u32[]{:S(2)}) collective-permute-start(bf16[512,1024]{1,0:T(8,128)(2,1)} %get-tuple-element.90), channel_id=1, source_target_pairs={{0,1},{1,0},{2,3},{3,2},{4,5},{5,4},{6,7},{7,6},{8,9},{9,8},{10,11... | collective-permute-start | bytes 3145736 | tf_op jit(solution)/shard_map/ppermute | solution.py:398
  192.3 41.1 %collective-permute-start.6 = (bf16[512,1024]{1,0:T(8,128)(2,1)S(1)}, bf16[512,1024]{1,0:T(8,128)(2,1)S(1)}, u32[]{:S(2)}, u32[]{:S(2)}) collective-permute-start(bf16[512,1024]{1,0:T(8,128)(2,1)S(1)} %fusion.26), channel_id=1, source_target_pairs={{0,2},{1,3},{2,0},{3,1},{4,6},{5,7},{6,4},{7,5},{8,10},{9,11},{10,... | collective-permute-start | bytes 3145736 | tf_op jit(solution)/shard_map/ppermute | solution.py:400
  238.9 25.1 %collective-permute-start.8 = (bf16[512,1024]{1,0:T(8,128)(2,1)S(1)}, bf16[512,1024]{1,0:T(8,128)(2,1)}, u32[]{:S(2)}, u32[]{:S(2)}) collective-permute-start(bf16[512,1024]{1,0:T(8,128)(2,1)S(1)} %multiply_convert_fusion.1), channel_id=1, source_target_pairs={{0,2},{1,3},{2,0},{3,1},{4,6},{5,7},{6,4},{7,5},{8,10},{9,11},{10,... | collective-permute-start | bytes 3145736 | tf_op jit(solution)/shard_map/ppermute | solution.py:373
  239.3 33.5 %collective-permute-start.7 = (bf16[512,1024]{1,0:T(8,128)(2,1)S(1)}, bf16[512,1024]{1,0:T(8,128)(2,1)}, u32[]{:S(2)}, u32[]{:S(2)}) collective-permute-start(bf16[512,1024]{1,0:T(8,128)(2,1)S(1)} %multiply_convert_fusion.1), channel_id=1, source_target_pairs={{0,1},{1,0},{2,3},{3,2},{4,5},{5,4},{6,7},{7,6},{8,9},{9,8},{10,11... | collective-permute-start | bytes 3145736 | tf_op jit(solution)/shard_map/ppermute | solution.py:374
  264.0 11.5 %collective-permute-start.9 = (bf16[512,1024]{1,0:T(8,128)(2,1)}, bf16[512,1024]{1,0:T(8,128)(2,1)}, u32[]{:S(2)}, u32[]{:S(2)}) collective-permute-start(bf16[512,1024]{1,0:T(8,128)(2,1)} %collective-permute-done.8), channel_id=1, source_target_pairs={{0,1},{1,0},{2,3},{3,2},{4,5},{5,4},{6,7},{7,6},{8,9},{9,8},{10,11... | collective-permute-start | bytes 3145736 | tf_op jit(solution)/shard_map/ppermute | solution.py:375
  313.9 2.9 collective-permute-start.11
  314.4 3.8 collective-permute-start.10
  317.1 25.5 %collective-permute-start.12 = (bf16[512,1024]{1,0:T(8,128)(2,1)S(1)}, bf16[512,1024]{1,0:T(8,128)(2,1)S(1)}, u32[]{:S(2)}, u32[]{:S(2)}) collective-permute-start(bf16[512,1024]{1,0:T(8,128)(2,1)S(1)} %fusion.24), channel_id=1, source_target_pairs={{0,2},{1,3},{2,0},{3,1},{4,6},{5,7},{6,4},{7,5},{8,10},{9,11},{10,... | collective-permute-start | bytes 3145736 | tf_op jit(solution)/shard_map/ppermute | solution.py:400
  349.6 24.7 %collective-permute-start.14 = (bf16[512,1024]{1,0:T(8,128)(2,1)S(1)}, bf16[512,1024]{1,0:T(8,128)(2,1)}, u32[]{:S(2)}, u32[]{:S(2)}) collective-permute-start(bf16[512,1024]{1,0:T(8,128)(2,1)S(1)} %get-tuple-element.77), channel_id=1, source_target_pairs={{0,2},{1,3},{2,0},{3,1},{4,6},{5,7},{6,4},{7,5},{8,10},{9,11},{10,... | collective-permute-start | bytes 3145736 | tf_op jit(solution)/shard_map/ppermute | solution.py:373
  349.9 44.0 %collective-permute-start.13 = (bf16[512,1024]{1,0:T(8,128)(2,1)S(1)}, bf16[512,1024]{1,0:T(8,128)(2,1)}, u32[]{:S(2)}, u32[]{:S(2)}) collective-permute-start(bf16[512,1024]{1,0:T(8,128)(2,1)S(1)} %get-tuple-element.77), channel_id=1, source_target_pairs={{0,1},{1,0},{2,3},{3,2},{4,5},{5,4},{6,7},{7,6},{8,9},{9,8},{10,11... | collective-permute-start | bytes 3145736 | tf_op jit(solution)/shard_map/ppermute | solution.py:374
  374.3 22.1 %collective-permute-start.15 = (bf16[512,1024]{1,0:T(8,128)(2,1)}, bf16[512,1024]{1,0:T(8,128)(2,1)}, u32[]{:S(2)}, u32[]{:S(2)}) collective-permute-start(bf16[512,1024]{1,0:T(8,128)(2,1)} %collective-permute-done.14), channel_id=1, source_target_pairs={{0,1},{1,0},{2,3},{3,2},{4,5},{5,4},{6,7},{7,6},{8,9},{9,8},{10,11... | collective-permute-start | bytes 3145736 | tf_op jit(solution)/shard_map/ppermute | solution.py:375
  405.2 229.3 %reduce-scatter.8.cloned.1.call-start = ((), (), s32[]{:S(2)}) async-start(), calls=%async_computation.8 | async-start | bytes 5308416 | tf_op jit(solution)/shard_map/reduce_scatter | solution.py:484
  414.4 8.4 %collective-permute-start.17 = (bf16[512,1024]{1,0:T(8,128)(2,1)}, bf16[512,1024]{1,0:T(8,128)(2,1)}, u32[]{:S(2)}, u32[]{:S(2)}) collective-permute-start(bf16[512,1024]{1,0:T(8,128)(2,1)} %get-tuple-element.87), channel_id=1, source_target_pairs={{0,1},{1,0},{2,3},{3,2},{4,5},{5,4},{6,7},{7,6},{8,9},{9,8},{10,11... | collective-permute-start | bytes 3145736 | tf_op jit(solution)/shard_map/ppermute | solution.py:397
  422.1 177.9 %slice-start = ((s8[6291456]{0:T(1024)(128)(4,1)}), s8[2097152]{0:T(1024)(128)(4,1)S(1)}, s32[]{:S(2)}) async-start(s8[6291456]{0:T(1024)(128)(4,1)} %bitcast.111), calls=%async_computation.9 | async-start | bytes 4194304
  422.1 309.1 %reduce-scatter.4.cloned.1.call-start = ((), (), s32[]{:S(2)}) async-start(), calls=%async_computation.6 | async-start | bytes 2359296 | tf_op jit(solution)/shard_map/reduce_scatter | solution.py:521
  422.2 51.2 %collective-permute-start.16 = (bf16[512,1024]{1,0:T(8,128)(2,1)}, bf16[512,1024]{1,0:T(8,128)(2,1)}, u32[]{:S(2)}, u32[]{:S(2)}) collective-permute-start(bf16[512,1024]{1,0:T(8,128)(2,1)} %get-tuple-element.86), channel_id=1, source_target_pairs={{0,1},{1,0},{2,3},{3,2},{4,5},{5,4},{6,7},{7,6},{8,9},{9,8},{10,11... | collective-permute-start | bytes 3145736 | tf_op jit(solution)/shard_map/ppermute | solution.py:398
  425.3 48.0 %collective-permute-start.18 = (bf16[512,1024]{1,0:T(8,128)(2,1)S(1)}, bf16[512,1024]{1,0:T(8,128)(2,1)}, u32[]{:S(2)}, u32[]{:S(2)}) collective-permute-start(bf16[512,1024]{1,0:T(8,128)(2,1)S(1)} %fusion.20), channel_id=1, source_target_pairs={{0,2},{1,3},{2,0},{3,1},{4,6},{5,7},{6,4},{7,5},{8,10},{9,11},{10,... | collective-permute-start | bytes 3145736 | tf_op jit(solution)/shard_map/ppermute | solution.py:400
  425.7 174.2 %slice-start.1 = ((s8[6291456]{0:T(1024)(128)(4,1)}), s8[4194304]{0:T(1024)(128)(4,1)S(1)}, s32[]{:S(2)}) async-start(s8[6291456]{0:T(1024)(128)(4,1)} %bitcast.111), calls=%async_computation.10 | async-start | bytes 8388608
  479.8 120.2 %collective-permute-start.19 = (bf16[2048,512]{1,0:T(8,128)(2,1)S(1)}, bf16[2048,512]{1,0:T(8,128)(2,1)S(1)}, u32[]{:S(2)}, u32[]{:S(2)}) collective-permute-start(bf16[2048,512]{1,0:T(8,128)(2,1)S(1)} %pad_maximum_fusion.8), channel_id=1, source_target_pairs={{4,0},{5,1},{6,2},{7,3},{12,8},{13,9},{14,10},{15,11},{20,16},{21,... | collective-permute-start | bytes 6291464 | tf_op jit(solution)/shard_map/ppermute | solution.py:21
  624.1 4.1 collective-permute-start.21
  624.1 14.5 %collective-permute-start.20 = (bf16[512,1024]{1,0:T(8,128)(2,1)}, bf16[512,1024]{1,0:T(8,128)(2,1)}, u32[]{:S(2)}, u32[]{:S(2)}) collective-permute-start(bf16[512,1024]{1,0:T(8,128)(2,1)} %get-tuple-element.84), channel_id=1, source_target_pairs={{0,1},{1,0},{2,3},{3,2},{4,5},{5,4},{6,7},{7,6},{8,9},{9,8},{10,11... | collective-permute-start | bytes 3145736 | tf_op jit(solution)/shard_map/ppermute | solution.py:398
  630.9 25.5 %collective-permute-start.22 = (bf16[512,1024]{1,0:T(8,128)(2,1)}, bf16[512,1024]{1,0:T(8,128)(2,1)}, u32[]{:S(2)}, u32[]{:S(2)}) collective-permute-start(bf16[512,1024]{1,0:T(8,128)(2,1)} %fusion.18), channel_id=1, source_target_pairs={{0,2},{1,3},{2,0},{3,1},{4,6},{5,7},{6,4},{7,5},{8,10},{9,11},{10,... | collective-permute-start | bytes 3145736 | tf_op jit(solution)/shard_map/ppermute | solution.py:400
  (46 other events, 1062.2 us)
Sparse Core Ops, SparseCore 0:
  10.8 52.2 all-gather.4
  65.7 92.2 all-gather.6
  159.6 68.7 all-gather.8
  405.3 88.9 reduce-scatter.5
  498.2 105.4 reduce-scatter.7
  613.1 93.3 reduce-scatter.3
